TPU v7x, 256 devices: a whole 4x4x8 slice. The times are simulated.
256 devices in a mesh: expert: 16 (over z, core), tensor: 16 (over y, x).
Axes of the slice: x: 4, y: 4, z: 8, core: 2. Of those that a mesh axis runs over, the one named last changes fastest.
Arguments:
- queries: bfloat16 [96, 2, 6144], P('expert'), may hold values from -20 to 20
- new_kv: bfloat16 [2, 96, 2, 1024], P(None, 'expert'), may hold values from -4 to 4
- cache: bfloat16 [2, 96, 8, 4096, 128], P(None, 'expert', None, 'tensor'), may hold values from -4 to 4
- residual: bfloat16 [96, 2, 6144], P('expert'), may hold values from -16 to 16
- w_out: bfloat16 [6144, 6144], P('tensor'), may hold values from -0.078125 to 0.078125
- norm_gain: float32 [6144], replicated, may hold values from 0.1 to 1.9
- routes: int32 [96, 2, 4], P('expert'), may hold values from 0 to 7, all different within a row; in each aligned block of 12 rows (0 to 11, 12 to 23, ..., all dimensions but the last counted through in order) at most 9 rows name the same one
- route_weight: float32 [96, 2, 4], P('expert'), may hold values from 0.1 to 0.6
- w_in: bfloat16 [16, 6144, 2, 2688], P('expert', None, None, 'tensor'), may hold values from -0.078125 to 0.078125
- w_down: bfloat16 [16, 2688, 6144], P('expert', 'tensor'), may hold values from -0.109375 to 0.109375
Outputs:
- mixed: bfloat16 [96, 2, 6144], P('expert', None, 'tensor')
Inputs may be any that keep to these rules, and one draw needn't show every extreme that they name: `routes`: in each aligned block of 12 tokens (the rows of one index of expert) each expert is named at most 9 times; the 4 experts of a token differ.
All inputs are finite; a program needn't handle non-finite values.
Results may differ from a plain program's by a relative error of at most 0.014.
Values may be sent and summed in bfloat16 or wider, within the bound.
A program may use at most 128 MiB of HBM per device.

v0:
```python
import jax
import jax.numpy as jnp
from jax import lax
from jax.sharding import PartitionSpec as P

D = 6144
HEADS = 48
KV = 8
HD = 128
EXPERTS = 8
TOP = 4
CAP = 9


norm_epsilon = 1e-05


def merged_2(value, axis, join):
    pieces = jax.tree.map(lambda part: lax.all_gather(part, axis), value)
    head = jax.tree.map(lambda part: part[0], pieces)
    tail = jax.tree.map(lambda part: part[1:], pieces)
    total, _ = lax.scan(lambda total, section: (join(total, section), None), head, tail)
    return total


def partial_softmax(query_heads, key_rows, value_rows, allowed):
    scores = jnp.einsum(
        "rskgh,rklh->rskgl", query_heads, key_rows, preferred_element_type=jnp.float32
    )
    scores = scores * query_heads.shape[-1] ** (-0.5)
    if allowed is not None:
        scores = jnp.where(allowed[None, :, None, None, :], scores, -jnp.inf)
    row_max = jnp.max(scores, axis=-1)
    weights = jnp.exp(scores - row_max[..., None])
    row_total = jnp.sum(weights, axis=-1)
    weighted = jnp.einsum(
        "rskgl,rklh->rskgh",
        weights.astype(jnp.bfloat16),
        value_rows,
        preferred_element_type=jnp.float32,
    )
    return (row_max, row_total, weighted)


def join_parts(first, second):
    larger = jnp.maximum(first[0], second[0])
    factor_first = jnp.exp(first[0] - larger)
    factor_second = jnp.exp(second[0] - larger)
    row_total = first[1] * factor_first + second[1] * factor_second
    weighted = first[2] * factor_first[..., None] + second[2] * factor_second[..., None]
    return (larger, row_total, weighted)


def route_tables(routes, route_weight, tokens):
    flat_routes = routes.reshape(-1)
    one_hot = (flat_routes[:, None] == jnp.arange(EXPERTS, dtype=jnp.int32)[None, :]).astype(
        jnp.int32
    )
    earlier = jnp.cumsum(one_hot, axis=0) - one_hot
    slot_index = jnp.sum(earlier * one_hot, axis=1)
    target = flat_routes * CAP + slot_index
    chosen = (jnp.arange(EXPERTS * CAP, dtype=jnp.int32)[:, None] == target[None, :]).reshape(
        EXPERTS * CAP, tokens, TOP
    )
    dispatch_table = jnp.sum(chosen.astype(jnp.float32), axis=2).astype(jnp.bfloat16)
    combine_table = jnp.sum(jnp.where(chosen, route_weight.reshape(1, tokens, TOP), 0.0), axis=2).T
    return (dispatch_table, combine_table)


def expert_rows(received, w_in, w_down):
    senders, capacity, features = received.shape
    flat_rows = received.reshape(senders * capacity, features)
    paired = w_in[0].reshape(features, -1)
    projected = jnp.dot(flat_rows, paired, preferred_element_type=jnp.float32)
    units = paired.shape[1] // 2
    expert_hidden = (jax.nn.silu(projected[:, :units]) * projected[:, units:]).astype(jnp.bfloat16)
    slab_output = jnp.dot(expert_hidden, w_down[0], preferred_element_type=jnp.float32)
    return slab_output.reshape(senders, capacity, features)


def body(queries, new_kv, cache, residual, w_out, norm_gain, routes, route_weight, w_in, w_down):
    rows, steps, ignored = queries.shape
    tokens = rows * steps
    groups = HEADS // KV
    query_heads = queries.reshape(rows, steps, KV, groups, HD)
    cached = partial_softmax(query_heads, cache[0], cache[1], None)
    fresh_keys = new_kv[0].reshape(rows, steps, KV, HD).transpose(0, 2, 1, 3)
    fresh_values = new_kv[1].reshape(rows, steps, KV, HD).transpose(0, 2, 1, 3)
    causal = jnp.arange(steps)[None, :] <= jnp.arange(steps)[:, None]
    fresh = partial_softmax(query_heads, fresh_keys, fresh_values, causal)
    tensor_count = lax.axis_size("tensor")
    tensor_place = lax.axis_index("tensor")
    heads_here = HEADS // tensor_count
    merged = merged_2(cached, "tensor", join_parts)
    row_max, row_total, weighted = join_parts(merged, fresh)
    attended = (weighted / row_total[..., None]).astype(jnp.bfloat16).reshape(tokens, HEADS * HD)
    attended = lax.dynamic_slice_in_dim(
        attended, tensor_place * heads_here * HD, heads_here * HD, 1
    )
    projected = jnp.dot(attended, w_out, preferred_element_type=jnp.float32)
    stream = residual.reshape(tokens, D).astype(jnp.float32)
    features_here = D // tensor_count
    dispatch_table, combine_table = route_tables(routes, route_weight, tokens)
    copies = lax.axis_size("expert") // EXPERTS
    hidden_state = stream + lax.psum(projected, "tensor")
    average = jnp.mean(hidden_state, axis=1, keepdims=True)
    variance = jnp.mean(jnp.square(hidden_state - average), axis=1, keepdims=True)
    normed = ((hidden_state - average) * lax.rsqrt(variance + norm_epsilon) * norm_gain).astype(
        jnp.bfloat16
    )
    kept_state = lax.dynamic_slice_in_dim(
        hidden_state, tensor_place * features_here, features_here, 1
    )
    outgoing = jnp.dot(dispatch_table, normed, preferred_element_type=jnp.float32).astype(
        jnp.bfloat16
    )
    outgoing = jnp.repeat(outgoing.reshape(EXPERTS, CAP, D), copies, axis=0)
    received = lax.all_to_all(outgoing, "expert", split_axis=0, concat_axis=0, tiled=True)
    slab_output = expert_rows(received, w_in, w_down)
    shares = lax.psum_scatter(slab_output, "tensor", scatter_dimension=2, tiled=True)
    returned = lax.all_to_all(shares, "expert", split_axis=0, concat_axis=0, tiled=True)
    summed = jnp.sum(returned.reshape(EXPERTS, copies, CAP, features_here), axis=1).reshape(
        EXPERTS * CAP, features_here
    )
    expert_mix = jnp.dot(
        combine_table, summed, precision=lax.Precision.HIGHEST, preferred_element_type=jnp.float32
    )
    return (kept_state + expert_mix).astype(jnp.bfloat16).reshape(rows, steps, features_here)


def solution(mesh):
    return jax.shard_map(
        body,
        mesh=mesh,
        in_specs=(
            P("expert", None, None),
            P(None, "expert", None, None),
            P(None, "expert", None, "tensor", None),
            P("expert", None, None),
            P("tensor", None),
            P(),
            P("expert", None, None),
            P("expert", None, None),
            P("expert", None, None, "tensor"),
            P("expert", "tensor", None),
        ),
        out_specs=P("expert", None, "tensor"),
        check_vma=False,
    )
```

profile of v0, /device:TPU:6, one launch (start us, length us, event | category | flops | bytes accessed | tf_op | source)
XLA Modules:
  0.0 422.0 jit_solution(1439065275210209484)
XLA Ops:
  6.5 1.2 reshape.85
  7.7 2.9 fusion.58
  10.7 2.5 fusion.20
  14.8 24.6 %all-gather.1 = f32[96,2,8,6]{2,1,3,0:T(2,128)S(1)} all-gather(f32[6,2,8,6]{2,1,3,0:T(2,128)S(1)} %copy.69), channel_id=3, replica_groups=mesh['expert'=16,'tensor'=16] {'tensor'}, dimensions={0}, use_global_device_ids=true | all-gather | bytes 39168 | tf_op jit(solution)/shard_map/all_gather | solution.py:19
  39.5 22.9 %all-gather = f32[96,2,8,6]{2,1,3,0:T(2,128)S(1)} all-gather(f32[6,2,8,6]{2,1,3,0:T(2,128)S(1)} %copy.68), channel_id=2, replica_groups=mesh['expert'=16,'tensor'=16] {'tensor'}, dimensions={0}, use_global_device_ids=true | all-gather | bytes 39168 | tf_op jit(solution)/shard_map/all_gather | solution.py:19
  62.4 0.9 slice.57
  63.5 1.0 fusion.59
  65.4 11.8 %all-gather.5.cloned.1.call-done = f32[96,2,8,6,128]{4,2,3,1,0:T(8,128)} async-done(((f32[6,2,8,6,128]{4,2,3,1,0:T(8,128)}), f32[96,2,8,6,128]{4,2,3,1,0:T(8,128)}) %all-gather.5.cloned.1.call-update) | async-done | bytes 4718608 | tf_op jit(solution)/shard_map/all_gather | solution.py:19
  77.2 1.0 slice.56
  78.3 4.6 %slice.59 = f32[90,2,8,6,128]{4,2,3,1,0:T(8,128)} slice(f32[96,2,8,6,128]{4,2,3,1,0:T(8,128)} %all-gather.5.cloned.1.call-done), slice={[6:96], [0:2], [0:8], [0:6], [0:128]} | slice | bytes 8847360 | tf_op jit(solution)/shard_map/slice | solution.py:21
  83.0 37.4 %while.14 = (s32[]{:T(128)}, f32[6,2,8,6]{2,1,3,0:T(2,128)S(1)}, f32[6,2,8,6]{2,1,3,0:T(2,128)S(1)}, f32[6,2,8,6,128]{4,3,2,1,0:T(8,128)S(1)}, f32[15,6,2,8,6]{3...) while((s32[]{:T(128)}, f32[6,2,8,6]{2,1,3,0:T(2,128)S(1)}, ...), condition=%wide.region_3.4_spmd, body=%wide.region_2.3_spmd.sunk | while | flops 224642 | bytes 1506917 | solution.py:22
  83.0 0.9 fusion.69
  84.1 1.0 constant_dynamic-slice_fusion.2
  85.5 0.9 fusion.69
  86.6 1.0 constant_dynamic-slice_fusion.2
  88.0 0.9 fusion.69
  89.1 1.0 constant_dynamic-slice_fusion.2
  90.5 0.9 fusion.69
  91.6 1.0 constant_dynamic-slice_fusion.2
  93.0 0.9 fusion.69
  94.1 1.0 constant_dynamic-slice_fusion.2
  95.4 0.9 fusion.69
  96.6 1.0 constant_dynamic-slice_fusion.2
  97.9 0.9 fusion.69
  99.1 1.0 constant_dynamic-slice_fusion.2
  100.4 0.9 fusion.69
  101.6 1.0 constant_dynamic-slice_fusion.2
  104.1 1.0 constant_dynamic-slice_fusion.2
  106.6 1.0 constant_dynamic-slice_fusion.2
  107.9 0.9 fusion.69
  109.1 1.0 constant_dynamic-slice_fusion.2
  111.6 1.0 constant_dynamic-slice_fusion.2
  114.0 1.0 constant_dynamic-slice_fusion.2
  116.5 1.0 constant_dynamic-slice_fusion.2
  117.9 0.9 fusion.69
  119.0 1.0 constant_dynamic-slice_fusion.2
  121.5 3.8 fusion.50
  126.1 93.3 %all-reduce.2.cloned.1.call-done = f32[12,6144]{1,0:T(8,128)} async-done(((f32[12,6144]{1,0:T(8,128)}), f32[12,6144]{1,0:T(8,128)}) %all-reduce.2.cloned.1.call-update) | async-done | bytes 294928 | tf_op jit(solution)/shard_map/psum | solution.py:105
  219.4 1.2 fusion.55
  221.3 1.6 reshape.87
  222.8 1.8 broadcast_in_dim.50
  224.6 79.2 %all_to_all.10 = bf16[16,9,6144]{2,1,0:T(8,128)(2,1)} all-to-all(bf16[16,9,6144]{2,1,0:T(8,128)(2,1)S(1)} %bitcast.103), channel_id=1, replica_groups=mesh['expert'=16,'tensor'=16] {'expert'}, dimensions={0} | all-to-all | bytes 3538944 | tf_op jit(solution)/shard_map/all_to_all | solution.py:118
  303.8 3.2 reshape.89
  307.0 4.3 %fusion.60 = f32[144,336]{1,0:T(8,128)S(1)} fusion(bf16[144,6144]{1,0:T(8,128)(2,1)} %reshape.89, bf16[6144,336]{0,1:T(8,128)(2,1)} %bitcast.105), kind=kOutput, calls=%fused_computation.78 | convolution fusion | flops 594542592 | bytes 6091776 | tf_op jit(solution)/shard_map/dot_general | solution.py:74
  311.5 2.4 fusion.10
  313.9 79.1 %reduce-scatter.2.cloned.1.call-done = f32[16,9,384]{2,0,1:T(8,128)} async-done(((f32[16,9,6144]{2,0,1:T(8,128)}), f32[16,9,384]{2,0,1:T(8,128)}) %reduce-scatter.2.cloned.1.call-update) | async-done | bytes 221200 | tf_op jit(solution)/shard_map/reduce_scatter | solution.py:120
  393.0 1.0 copy.83
  394.0 20.6 %all_to_all.11 = f32[16,9,384]{2,1,0:T(8,128)S(1)} all-to-all(f32[16,9,384]{2,1,0:T(8,128)S(1)} %copy.83), channel_id=1, replica_groups=mesh['expert'=16,'tensor'=16] {'expert'}, dimensions={0} | all-to-all | bytes 442368 | tf_op jit(solution)/shard_map/all_to_all | solution.py:121
  (112 shorter events, 20.1 us)
Async XLA Ops:
  6.5 304.9 %copy-start = (bf16[1,168,6144]{2,1,0:T(8,128)(2,1)S(1)}, bf16[1,168,6144]{2,1,0:T(8,128)(2,1)}, u32[]{:S(2)}) copy-start(bf16[1,168,6144]{2,1,0:T(8,128)(2,1)} %param.21) | copy-start | bytes 6193156
  6.5 70.7 %all-gather.5.cloned.1.call-start = ((), (), s32[]{:S(2)}) async-start(), calls=%async_computation.5 | async-start | bytes 5013504 | tf_op jit(solution)/shard_map/all_gather | solution.py:19
  13.2 50.1 %copy-start.5 = (s32[6,2,4]{0,2,1:T(4,128)S(1)}, s32[6,2,4]{0,2,1:T(4,128)}, u32[]{:S(2)}) copy-start(s32[6,2,4]{0,2,1:T(4,128)} %param.18) | copy-start | bytes 580
  13.2 50.3 %copy-start.7 = (bf16[2,6,2,1024]{3,2,1,0:T(2,128)(2,1)S(1)}, bf16[2,6,2,1024]{3,2,1,0:T(2,128)(2,1)}, u32[]{:S(2)}) copy-start(bf16[2,6,2,1024]{3,2,1,0:T(2,128)(2,1)} %param.13) | copy-start | bytes 147460
  14.1 205.3 %all-reduce.2.cloned.1.call-start = ((), (), s32[]{:S(2)}) async-start(), calls=%async_computation.3 | async-start | bytes 786432 | tf_op jit(solution)/shard_map/psum | solution.py:105
  64.5 0.6 copy-start.2
  83.0 37.7 %copy-start.3 = (f32[6,2,8,6,2]{3,4,1,2,0:T(2,128)S(1)}, f32[6,2,8,6,2]{3,4,1,2,0:T(2,128)}, u32[]{:S(2)}) copy-start(f32[6,2,8,6,2]{3,4,1,2,0:T(2,128)} %copy-done.2) | copy-start | bytes 13828
  121.2 4.3 %copy-start.6 = (f32[6,2,4]{0,2,1:T(4,128)S(1)}, f32[6,2,4]{0,2,1:T(4,128)}, u32[]{:S(2)}) copy-start(f32[6,2,4]{0,2,1:T(4,128)} %param.19) | copy-start | bytes 580
  121.2 4.7 %copy-start.1 = (bf16[6,2,6144]{2,1,0:T(2,128)(2,1)S(1)}, bf16[6,2,6144]{2,1,0:T(2,128)(2,1)}, u32[]{:S(2)}) copy-start(bf16[6,2,6144]{2,1,0:T(2,128)(2,1)} %param.15) | copy-start | bytes 442372
  121.5 99.4 %copy-start.4 = (f32[6144]{0:T(1024)S(1)}, f32[6144]{0:T(1024)}, u32[]{:S(2)}) copy-start(f32[6144]{0:T(1024)} %param.17) | copy-start | bytes 73732
  125.3 267.7 %reduce-scatter.2.cloned.1.call-start = ((), (), s32[]{:S(2)}) async-start(), calls=%async_computation.4 | async-start | bytes 3760128 | tf_op jit(solution)/shard_map/reduce_scatter | solution.py:120
Sparse Core Ops, SparseCore 0:
  14.2 63.0 all-gather.4
  125.4 93.9 all-reduce.1
  314.0 78.9 reduce-scatter.1
where the time goes:
time: 426 us; the launch traced here: 422 us
  waiting for transfers between devices  184 us (43%)
  blocking collectives  147 us (35%)
  local copies, waits for them, and re-layouts  38 us (9%)
  other arithmetic  20.6 us (5%)
  matrix products  18.1 us (4%)
  between operations  13.4 us (3%)
    psum x1, waiting for transfers between devices, body(): hidden_state = stream + lax.psum(projected, 'tensor')  93.3 us
    all_to_all x1, blocking collectives, body(): lax.all_to_all(outgoing, 'expert', split_axis=0, concat_axis=0, tiled=True)  79.2 us
    reduce_scatter x1, waiting for transfers between devices, body(): lax.psum_scatter(slab_output, 'tensor', scatter_dimension=2, tiled=True)  79.1 us
    all_gather x2, blocking collectives, merged_2(): pieces = jax.tree.map(lambda part: lax.all_gather(part, axis), value)  47.5 us
    all_to_all x1, blocking collectives, body(): lax.all_to_all(shares, 'expert', split_axis=0, concat_axis=0, tiled=True)  20.6 us
    dynamic_slice x15, local copies, waits for them, and re-layouts, merged_2(): lax.scan(lambda total, section: (join(total, section), None), head, tail)  14.7 us
    add x16, other arithmetic, join_parts(): row_total = first[1] * factor_first + second[1] * factor_second  13 us
    all_gather x1, waiting for transfers between devices, merged_2(): pieces = jax.tree.map(lambda part: lax.all_gather(part, axis), value)  11.8 us
  transfers between devices with their start and end apart: 3, of which 3 were waited for; matrix products, arithmetic and copies ran while one was open for 1% of the time, Pallas kernels for 0%

commit v1 on v0

v1 whole, which is shorter than its diff:
```python
import jax
import jax.numpy as jnp
from jax import lax
from jax.experimental import pallas as pl
from jax.experimental.pallas import tpu as pltpu
from jax.sharding import PartitionSpec as P

D = 6144
HEADS = 48
KV = 8
HD = 128
EXPERTS = 8
TOP = 4
CAP = 9
ROWS = 6
STEPS = 2
KEYS = 256
UNITS = 168
PART = 384
PACK = 80
EPS = 1e-05
BF = jnp.bfloat16
F32 = jnp.float32
MESH = pl.DeviceIdType.MESH
NT = (((1,), (1,)), ((), ()))
TN = (((0,), (0,)), ((), ()))


def wrap(value, size):
    return lax.rem(value + size, size)


def iota(shape, dim):
    return lax.broadcasted_iota(jnp.int32, shape, dim)


def dot(a, b, dims=None):
    if dims is None:
        return jnp.dot(a, b, preferred_element_type=F32)
    return lax.dot_general(a, b, dims, preferred_element_type=F32)


def kernel(
    q_ref, nkv_ref, cache_ref, res_ref, wout_hbm, gain_ref, routes_ref, rw_ref, win_hbm, wdn_hbm,
    out_ref,
    kv, wout, win, wdn,
    a_send, a_recv, stat, fcol, att, proj, b_send, b_recv,
    state, z_send, z_recv, xall, acc, vacc, hid,
    q_send, q_recv, g_send, g_recv, chip, m_send, m_recv, y_send, y_recv,
    kv_sem, w_sem,
    a_ss, a_rs, b_ss, b_rs, z_ss, z_rs, x1_ss, x1_rs, x2_ss, x2_rs, xp_ss, xp_rs,
    q_ss, q_rs, g_ss, g_rs, m_ss, m_rs, y_ss, y_rs,
):
    b = lax.axis_index("expert")
    t = lax.axis_index("tensor")
    z, c = lax.div(b, 2), lax.rem(b, 2)
    y, x = lax.div(t, 4), lax.rem(t, 4)
    partner = 2 * z + 1 - c
    m = (1 - c) * x + c * y
    g = (1 - c) * y + c * x

    def place(core, group, member):
        return (1 - core) * (4 * group + member) + core * (4 * member + group)

    def plane_peer(i, sign):
        return 4 * wrap(y + sign * lax.div(i, 4), 4) + wrap(x + sign * lax.rem(i, 4), 4)

    def remote(src, dst, ss, rs, dev):
        return pltpu.make_async_remote_copy(
            src_ref=src, dst_ref=dst, send_sem=ss, recv_sem=rs, device_id=dev, device_id_type=MESH
        )

    def loop(lo, hi, fn):
        def step(i, carry):
            fn(i)
            return carry
        lax.fori_loop(lo, hi, step, 0)

    def load_row(r):
        return [
            pltpu.make_async_copy(cache_ref.at[s, r], kv.at[s, r], kv_sem.at[s, r]) for s in range(2)
        ]

    def start_row(r):
        for copy in load_row(r):
            copy.start()

    loop(0, ROWS, start_row)
    w_copies = [
        pltpu.make_async_copy(wout_hbm, wout, w_sem.at[0]),
        pltpu.make_async_copy(win_hbm, win, w_sem.at[1]),
        pltpu.make_async_copy(wdn_hbm, wdn, w_sem.at[2]),
    ]
    for copy in w_copies:
        copy.start()

    barrier = pltpu.get_barrier_semaphore()

    def greet(dev):
        pl.semaphore_signal(barrier, inc=1, device_id=dev, device_id_type=MESH)

    loop(1, 16, lambda i: greet((b, plane_peer(i, 1))))
    loop(1, 8, lambda d: greet((2 * wrap(z + d, 8) + c, t)))
    greet((partner, t))

    first = t == 0
    row_id = iota((128, 16), 0)
    key_id = iota((128, 16), 1)
    fresh_ok = (
        (lax.div(row_id, 16) == lax.div(key_id, 2))
        & (lax.rem(key_id, 2) <= lax.rem(row_id, 2))
        & (jnp.broadcast_to(t, (128, 16)) == 0)
    )
    lane = iota((128, 128), 1)
    stat[...] = jnp.zeros_like(stat)

    def attend_pair(pair):
        halves = []
        for half in range(2):
            r = 2 * pair + half
            k_copy, v_copy = load_row(r)
            k_copy.wait()
            qr = q_ref[r]
            scores = jnp.concatenate(
                [dot(qr[16 * k : 16 * k + 16], kv[0, r, k], NT) for k in range(KV)], axis=0
            ) * (HD**-0.5)
            extra = dot(qr, nkv_ref[0, r], NT) * (HD**-0.5)
            extra = jnp.where(fresh_ok, extra, -jnp.inf)
            top = jnp.maximum(
                jnp.max(scores, axis=1, keepdims=True), jnp.max(extra, axis=1, keepdims=True)
            )
            top = jnp.ceil(top * 0.25) * 4.0
            weights = jnp.exp(scores - top)
            extra = jnp.exp(extra - top)
            total = jnp.sum(weights, axis=1, keepdims=True) + jnp.sum(extra, axis=1, keepdims=True)
            low = weights.astype(BF)
            v_copy.wait()
            mixed = jnp.concatenate(
                [dot(low[16 * k : 16 * k + 16], kv[1, r, k]) for k in range(KV)], axis=0
            ) + dot(extra.astype(BF), nkv_ref[1, r])
            stat[...] = jnp.where(lane == r, top, jnp.where(lane == 8 + r, total, stat[...]))
            halves.append(mixed.reshape(16, 8, 128))
        a_send[:, pl.ds(pl.multiple_of(16 * pair, 16), 16), :] = jnp.concatenate(
            halves, axis=1
        ).astype(BF)

    loop(0, 3, attend_pair)
    table = jnp.transpose(stat[...])[0:16, :].astype(BF)
    a_send[:, 48:64, :] = jnp.broadcast_to(table[None], (16, 16, 128))
    a_recv[t] = a_send[t]
    pl.semaphore_wait(barrier, 23)

    def a_copy(i):
        to = plane_peer(i, 1)
        return remote(a_send.at[to], a_recv.at[t], a_ss.at[i], a_rs.at[i], (b, to))

    loop(1, 16, lambda i: a_copy(i).start())

    slot_lane = iota((16, 128), 1)
    token_row = iota((16, 128), 0)
    lane_expert = lax.div(slot_lane, 16)
    chosen = jnp.zeros((16, 128), F32)
    factor = jnp.zeros((16, 128), F32)
    for k in range(TOP):
        hit = routes_ref[:, k : k + 1] == lane_expert
        chosen = jnp.where(hit, 1.0, chosen)
        factor = jnp.where(hit, rw_ref[:, k : k + 1], factor)
    below = (iota((16, 16), 1) < iota((16, 16), 0)).astype(BF)
    earlier = dot(below, chosen.astype(BF))
    here = (chosen > 0.5) & (earlier.astype(jnp.int32) == lax.rem(slot_lane, 16))
    dispatch = jnp.where(here, 1.0, 0.0).astype(BF)
    combine = jnp.where(here, factor, 0.0)
    combine_high = combine.astype(BF)
    combine_low = (combine - combine_high.astype(F32)).astype(BF)
    mine = pl.ds(pl.multiple_of(t * PART, 128), PART)
    res_sum = jnp.sum(res_ref[...].astype(F32), axis=1, keepdims=True)
    gain_mine = gain_ref[:, mine]
    pack_row, pack_lane = iota((PACK, 128), 0), iota((PACK, 128), 1)
    packing = jnp.where(
        (pack_row == CAP * lax.div(pack_lane, 16) + lax.rem(pack_lane, 16))
        & (lax.rem(pack_lane, 16) < CAP),
        1.0,
        0.0,
    ).astype(BF)
    acc[...] = jnp.zeros_like(acc)
    vacc[...] = jnp.zeros_like(vacc)
    att[...] = jnp.zeros_like(att)
    w_copies[0].wait()

    loop(1, 16, lambda i: a_copy(i).wait_recv())

    stats = a_recv[:, 48:64, :].astype(F32)
    tops, totals = stats[:, 0:8], stats[:, 8:16]
    top = jnp.max(tops, axis=0, keepdims=True)
    scale = jnp.exp(tops - top)
    whole = jnp.sum(scale * totals, axis=0, keepdims=True)
    scale = scale / jnp.maximum(whole, 1e-30)
    fcol[...] = jnp.transpose(scale.reshape(128, 128))
    columns = fcol[pl.ds(pl.multiple_of(8 * t, 8), 8), :]
    for pair in range(3):
        both = a_recv[:, 16 * pair : 16 * pair + 16, :].astype(F32)
        for half in range(2):
            r = 2 * pair + half
            joined = jnp.zeros((8, 128), F32)
            for s in range(16):
                joined += both[s, 8 * half : 8 * half + 8] * columns[:, 8 * s + r : 8 * s + r + 1]
            for h in range(3):
                att[2 * r : 2 * r + 2, 128 * h : 128 * h + 128] = joined[2 * h : 2 * h + 2]

    attended = att[...].astype(BF)
    proj_sum = jnp.zeros((16, 1), F32)
    for s in range(16):
        part = dot(attended, wout[:, PART * s : PART * s + PART])
        proj[s] = part
        proj_sum = proj_sum + jnp.sum(part, axis=1, keepdims=True)
    diagonal = jnp.sum(jnp.where(token_row == slot_lane, proj_sum, 0.0), axis=0, keepdims=True)
    high = diagonal.astype(BF).astype(F32)
    low = diagonal - high
    head = jnp.where(token_row == 12, high, jnp.where(token_row == 13, low, 0.0))

    def b_fill(s):
        part = proj[s]
        b_send[s] = (
            part + jnp.concatenate([head, jnp.zeros((16, PART - 128), F32)], axis=1)
        ).astype(BF)

    def b_copy(i):
        to = plane_peer(i, 1)
        return remote(b_send.at[to], b_recv.at[t], b_ss.at[i], b_rs.at[i], (b, to))

    def b_step(i):
        b_fill(plane_peer(i, 1))
        b_copy(i).start()

    loop(1, 16, b_step)
    b_fill(t)
    b_recv[t] = b_send[t]
    loop(1, 16, lambda i: b_copy(i).wait_recv())

    summed = jnp.sum(b_recv[...].astype(F32), axis=0)
    spread = jnp.where(token_row == slot_lane, summed[12:13, 0:128] + summed[13:14, 0:128], 0.0)
    mean = (jnp.sum(spread, axis=1, keepdims=True) + res_sum) * (1.0 / D)
    real = iota((16, PART), 0) < ROWS * STEPS
    hidden = jnp.where(real, summed + res_ref[:, mine].astype(F32), 0.0)
    state[...] = hidden
    scaled = jnp.where(real, (hidden - mean) * gain_mine, 0.0).astype(BF)

    z_send[...] = dot(dispatch, scaled, TN).astype(BF).reshape(EXPERTS, 16, PART)
    z_recv[z] = z_send[z]

    def z_copy(d):
        to = wrap(z + d, 8)
        return remote(z_send.at[to], z_recv.at[z], z_ss.at[d], z_rs.at[d], (2 * to + c, t))

    loop(1, 8, lambda d: z_copy(d).start())
    w_copies[1].wait()
    w_copies[2].wait()
    loop(1, 8, lambda d: z_copy(d).wait_recv())
    xall[c, t] = dot(packing, z_recv[...].reshape(128, PART)).astype(BF)

    def x1_copy(j):
        return remote(
            xall.at[c, t], xall.at[c, t], x1_ss.at[j], x1_rs.at[j], (b, place(c, g, wrap(m + j, 4)))
        )

    def x2_copy(j, d):
        s = place(c, g, wrap(m - j, 4))
        n = 4 * j + d
        return remote(
            xall.at[c, s], xall.at[c, s], x2_ss.at[n], x2_rs.at[n], (b, place(c, wrap(g + d, 4), m))
        )

    def xp_copy(j, d):
        s = place(c, wrap(g - d, 4), wrap(m - j, 4))
        n = 4 * j + d
        return remote(xall.at[c, s], xall.at[c, s], xp_ss.at[n], xp_rs.at[n], (partner, t))

    loop(1, 4, lambda j: x1_copy(j).start())
    loop(1, 4, lambda d: x2_copy(0, d).start())
    xp_copy(0, 0).start()

    def pass_on(j):
        x1_copy(j).wait_recv()
        loop(1, 4, lambda d: x2_copy(j, d).start())
        xp_copy(j, 0).start()

    loop(1, 4, pass_on)

    def multiply(core, side, s):
        rows = xall[core, s]
        cols = pl.ds(pl.multiple_of(s * PART, 128), PART)
        acc[side, 0] += dot(rows, win[0, :, cols], NT)
        acc[side, 1] += dot(rows, win[1, :, cols], NT)
        plain = rows.astype(F32) * (1.0 / gain_ref[:, cols])
        plain = plain * plain
        vacc[side] += plain[:, 0:128] + plain[:, 128:256] + plain[:, 256:384]

    def own_slice(n):
        d, j = lax.div(n, 4), lax.rem(n, 4)
        multiply(c, 0, place(c, wrap(g - d, 4), wrap(m - j, 4)))

    def partner_slice(n):
        d, j = lax.div(n, 4), lax.rem(n, 4)
        xp_copy(j, d).wait_recv()
        multiply(1 - c, 1, place(1 - c, wrap(m - d, 4), wrap(g - j, 4)))

    def gather_step(n):
        d, j = lax.div(n, 4), lax.rem(n, 4)
        x2_copy(j, d).wait_recv()
        xp_copy(j, d).start()
        own_slice(n)
        partner_slice(n - 4)

    loop(0, 4, own_slice)
    loop(4, 16, gather_step)
    loop(12, 16, partner_slice)

    for side in range(2):
        spread2 = jnp.sum(vacc[side], axis=1, keepdims=True) * (1.0 / D)
        inverse = lax.rsqrt(spread2 + EPS)
        gate, up = acc[side, 0] * inverse, acc[side, 1] * inverse
        hid[side] = (gate / (1.0 + jnp.exp(-gate)) * up).astype(BF)

    def slab(side, s):
        return dot(hid[side], wdn[:, pl.ds(pl.multiple_of(s * PART, 128), PART)])

    def q_copy(n):
        return remote(q_send.at[n], q_recv.at[n], q_ss.at[n], q_rs.at[n], (partner, t))

    def for_partner(n):
        d, j = 1 + lax.div(n, 4), lax.rem(n, 4)
        q_send[n] = slab(1, place(1 - c, wrap(m + d, 4), wrap(g + j, 4))).astype(BF)
        q_copy(n).start()

    def chip_sum(n):
        d, j = 1 + lax.div(n, 4), lax.rem(n, 4)
        own = slab(0, place(c, wrap(g + d, 4), wrap(m + j, 4)))
        q_copy(n).wait_recv()
        return own + q_recv[n].astype(F32)

    def g_copy(n):
        d = 1 + lax.div(n, 4)
        return remote(
            g_send.at[n], g_recv.at[n], g_ss.at[n], g_rs.at[n], (b, place(c, wrap(g + d, 4), m))
        )

    def down_step(n):
        for_partner(n)
        g_send[n - 4] = chip_sum(n - 4).astype(BF)
        g_copy(n - 4).start()

    def keep_step(n):
        chip[n - 12] = chip_sum(n)

    loop(0, 4, for_partner)
    loop(4, 16, down_step)
    loop(12, 16, keep_step)

    def m_copy(j):
        return remote(
            m_send.at[j], m_recv.at[j], m_ss.at[j], m_rs.at[j], (b, place(c, g, wrap(m + j, 4)))
        )

    def group_sum(j):
        for d in range(3):
            g_copy(4 * d + j).wait_recv()
        return (
            chip[j] + g_recv[j].astype(F32) + g_recv[4 + j].astype(F32) + g_recv[8 + j].astype(F32)
        )

    def member_step(j):
        m_send[j] = group_sum(j).astype(BF)
        m_copy(j).start()

    loop(1, 4, member_step)
    final = group_sum(0)
    loop(1, 4, lambda j: m_copy(j).wait_recv())
    for j in range(1, 4):
        final = final + m_recv[j].astype(F32)

    y_send[...] = dot(packing, final.astype(BF), TN).astype(BF).reshape(EXPERTS, 16, PART)
    y_recv[z] = y_send[z]

    def y_copy(d):
        to = wrap(z + d, 8)
        return remote(y_send.at[to], y_recv.at[z], y_ss.at[d], y_rs.at[d], (2 * to + c, t))

    loop(1, 8, lambda d: y_copy(d).start())

    loop(1, 16, lambda i: a_copy(i).wait_send())
    loop(1, 16, lambda i: b_copy(i).wait_send())
    loop(1, 8, lambda d: z_copy(d).wait_send())
    loop(1, 4, lambda j: x1_copy(j).wait_send())
    loop(0, 4, lambda j: loop(1, 4, lambda d: x2_copy(j, d).wait_send()))
    loop(0, 16, lambda n: xp_copy(lax.div(n, 4), lax.rem(n, 4)).wait_send())
    loop(0, 16, lambda n: q_copy(n).wait_send())
    loop(0, 12, lambda n: g_copy(n).wait_send())
    loop(1, 4, lambda j: m_copy(j).wait_send())

    loop(1, 8, lambda d: y_copy(d).wait_recv())
    returned = y_recv[...].reshape(128, PART)
    mix = dot(combine_high, returned) + dot(combine_low, returned)
    out_ref[...] = (state[...] + mix).astype(BF)
    loop(1, 8, lambda d: y_copy(d).wait_send())


def body(queries, new_kv, cache, residual, w_out, norm_gain, routes, route_weight, w_in, w_down):
    heads = queries.reshape(ROWS, STEPS, 16, 3, HD).transpose(0, 2, 3, 1, 4)
    heads = heads.reshape(ROWS, 16, 6, HD)
    heads = jnp.pad(heads, ((0, 0), (0, 0), (0, 2), (0, 0))).reshape(ROWS, 128, HD)
    fresh = new_kv.reshape(2, ROWS, STEPS, KV, HD).transpose(0, 1, 3, 2, 4)
    fresh = fresh.reshape(2, ROWS, 16, HD)
    stream = jnp.pad(residual.reshape(12, D), ((0, 4), (0, 0)))
    chosen = jnp.pad(routes.reshape(12, TOP), ((0, 4), (0, 0)), constant_values=-1)
    factors = jnp.pad(route_weight.reshape(12, TOP), ((0, 4), (0, 0)))
    w_in_t = w_in.transpose(0, 2, 3, 1).reshape(2, UNITS, D)
    w_down = w_down.reshape(UNITS, D)
    gain = norm_gain.reshape(1, D)
    vmem = pl.BlockSpec(memory_space=pltpu.VMEM)
    hbm = pl.BlockSpec(memory_space=pl.ANY)
    dma = pltpu.SemaphoreType.DMA
    out = pl.pallas_call(
        kernel,
        out_shape=jax.ShapeDtypeStruct((16, PART), BF),
        in_specs=[vmem, vmem, hbm, vmem, hbm, vmem, vmem, vmem, hbm, hbm],
        out_specs=vmem,
        scratch_shapes=[
            pltpu.VMEM((2, ROWS, KV, KEYS, HD), BF),
            pltpu.VMEM((PART, D), BF),
            pltpu.VMEM((2, UNITS, D), BF),
            pltpu.VMEM((UNITS, D), BF),
            pltpu.VMEM((16, 64, 128), BF),
            pltpu.VMEM((16, 64, 128), BF),
            pltpu.VMEM((128, 128), F32),
            pltpu.VMEM((128, 128), F32),
            pltpu.VMEM((16, PART), F32),
            pltpu.VMEM((16, 16, PART), F32),
            pltpu.VMEM((16, 16, PART), BF),
            pltpu.VMEM((16, 16, PART), BF),
            pltpu.VMEM((16, PART), F32),
            pltpu.VMEM((EXPERTS, 16, PART), BF),
            pltpu.VMEM((EXPERTS, 16, PART), BF),
            pltpu.VMEM((2, 16, PACK, PART), BF),
            pltpu.VMEM((2, 2, PACK, UNITS), F32),
            pltpu.VMEM((2, PACK, 128), F32),
            pltpu.VMEM((2, PACK, UNITS), BF),
            pltpu.VMEM((16, PACK, PART), BF),
            pltpu.VMEM((16, PACK, PART), BF),
            pltpu.VMEM((12, PACK, PART), BF),
            pltpu.VMEM((12, PACK, PART), BF),
            pltpu.VMEM((4, PACK, PART), F32),
            pltpu.VMEM((4, PACK, PART), BF),
            pltpu.VMEM((4, PACK, PART), BF),
            pltpu.VMEM((EXPERTS, 16, PART), BF),
            pltpu.VMEM((EXPERTS, 16, PART), BF),
            dma((2, ROWS)),
            dma((3,)),
            dma((16,)), dma((16,)),
            dma((16,)), dma((16,)),
            dma((8,)), dma((8,)),
            dma((4,)), dma((4,)),
            dma((16,)), dma((16,)),
            dma((16,)), dma((16,)),
            dma((16,)), dma((16,)),
            dma((12,)), dma((12,)),
            dma((4,)), dma((4,)),
            dma((8,)), dma((8,)),
        ],
        compiler_params=pltpu.CompilerParams(
            collective_id=0, has_side_effects=True, vmem_limit_bytes=48 * 1024 * 1024
        ),
        name="layer",
    )(heads, fresh, cache, stream, w_out, gain, chosen, factors, w_in_t, w_down)
    return out[:12].reshape(ROWS, STEPS, PART)


def solution(mesh):
    return jax.shard_map(
        body,
        mesh=mesh,
        in_specs=(
            P("expert", None, None),
            P(None, "expert", None, None),
            P(None, "expert", None, "tensor", None),
            P("expert", None, None),
            P("tensor", None),
            P(),
            P("expert", None, None),
            P("expert", None, None),
            P("expert", None, None, "tensor"),
            P("expert", "tensor", None),
        ),
        out_specs=P("expert", None, "tensor"),
        check_vma=False,
    )
```

time: 426 us -> 75.1 us (0.18)
  waiting for transfers between devices: 184 us -> 0 us
  blocking collectives: 147 us -> 0 us
  Pallas kernels: 0 us -> 66.4 us
  local copies, waits for them, and re-layouts: 38 us -> 7.48 us
  other arithmetic: 20.6 us -> 0 us
  matrix products: 18.1 us -> 0 us
  between operations: 13.4 us -> 0.06 us
    all_to_all x2 -> x0, blocking collectives: 99.8 us -> none  [the longest x1 79.2 us: body(): lax.all_to_all(outgoing, 'expert', split_axis=0, concat_axis=0, tiled=True)]
    psum x1 -> x0, waiting for transfers between devices: 93.3 us -> none  [body(): hidden_state = stream + lax.psum(projected, 'tensor')]
    reduce_scatter x1 -> x0, waiting for transfers between devices: 79.1 us -> none  [body(): lax.psum_scatter(slab_output, 'tensor', scatter_dimension=2, tiled=True)]
    pallas_call x0 -> x1, Pallas kernels: none -> 66.4 us  [body(): pl.pallas_call(kernel, out_shape=jax.ShapeDtypeStruct((16, PART), BF), in...]
    all_gather x2 -> x0, blocking collectives: 47.5 us -> none  [merged_2(): pieces = jax.tree.map(lambda part: lax.all_gather(part, axis), value)]
    dot_general x9 -> x0, matrix products: 18.1 us -> none  [the longest x1 4.27 us: expert_rows(): projected = jnp.dot(flat_rows, paired, preferred_element_type=jnp.float32)]
    add x32 -> x0, other arithmetic: 18.1 us -> none  [the longest x16 13 us: join_parts(): row_total = first[1] * factor_first + second[1] * factor_second]
    dynamic_slice x15 -> x0, local copies, waits for them, and re-layouts: 14.7 us -> none  [merged_2(): lax.scan(lambda total, section: (join(total, section), None), head, tail)]
  transfers between devices with their start and end apart: 3 -> 0, of which waited for: 3 -> 0; matrix products, arithmetic and copies ran while one was open for 1% -> 0% of each run, Pallas kernels for 0% -> 0%
where the time goes in v1:
time: 75.1 us; the launch traced here: 74 us
  Pallas kernels  66.4 us (88%)
  local copies, waits for them, and re-layouts  7.48 us (10%)
    pallas_call x1, Pallas kernels, body(): pl.pallas_call(kernel, out_shape=jax.ShapeDtypeStruct((16, PART), BF), in...  66.4 us
    unnamed x9, local copies, waits for them, and re-layouts  4.72 us

profile of v1, /device:TPU:6, one launch (start us, length us, event | category | flops | bytes accessed | tf_op | source)
XLA Modules:
  0.0 74.0 jit_solution(15720658960134692336)
XLA Ops:
  0.0 1.0 %reshape.36 = bf16[6,2,16,3,128]{4,3,2,1,0:T(4,128)(2,1)S(1)} reshape(bf16[6,2,6144]{2,1,0:T(2,128)(2,1)} %param.10) | data formatting | bytes 294912 | tf_op jit(solution)/shard_map/reshape | solution.py:408
  1.1 0.1 copy.20
  1.2 1.0 %reshape.41 = bf16[12,6144]{1,0:T(8,128)(2,1)S(1)} reshape(bf16[6,2,6144]{2,1,0:T(2,128)(2,1)} %param.13) | data formatting | bytes 294912 | tf_op jit(solution)/shard_map/reshape | solution.py:413
  2.2 0.8 %copy.18 = s32[6,2,4]{2,1,0:T(2,128)S(1)} copy(s32[6,2,4]{0,2,1:T(4,128)} %param.16) | data formatting | bytes 384 | tf_op args[6]
  3.0 0.8 %copy.19 = f32[6,2,4]{2,1,0:T(2,128)S(1)} copy(f32[6,2,4]{0,2,1:T(4,128)} %param.17) | data formatting | bytes 384 | tf_op args[7]
  3.8 0.0 copy-start
  3.8 1.6 %copy-done = bf16[1,168,6144]{2,1,0:T(8,128)(2,1)S(1)} copy-done((bf16[1,168,6144]{2,1,0:T(8,128)(2,1)S(1)}, bf16[1,168,6144]{2,1,0:T(8,128)(2,1)}, u32[]{:S(2)}) %copy-start) | copy-done | bytes 2064408
  5.4 0.0 copy-start.1
  5.4 0.8 %copy-done.1 = bf16[2,6,2,1024]{3,2,1,0:T(2,128)(2,1)S(1)} copy-done((bf16[2,6,2,1024]{3,2,1,0:T(2,128)(2,1)S(1)}, bf16[2,6,2,1024]{3,2,1,0:T(2,128)(2,1)}, u32[]{:S(2)}) %copy-start.1) | copy-done | bytes 49176
  6.2 0.0 copy-start.2
  6.2 0.7 copy-done.2
  6.9 66.4 %layer.1 = bf16[16,384]{1,0:T(8,128)(2,1)S(1)} custom-call(bf16[6,128,128]{2,1,0:T(8,128)(2,1)S(1)} %pad_bitcast_fusion.q_ref, bf16[2,6,16,128]{3,2,1,0:T(8,128)(2,1)S(1)} %bitcast.16, bf16[2,6,8,256,128]{4,3,2,1,0:T(8,128)(2,1)} %cache_ref.1, bf16[16,6144]{1,0:T(8,128)(2,1)S(1)} %pad.17.res_ref, bf16[384,6144]{1,0:T(8,128)(2,1)} %wout_hbm.1, ...), custom_call_target="tpu_custom_call" | custom-call | tf_op jit(solution)/shard_map/layer/pallas_call | solution.py:422
  73.4 0.6 reshape.47
  (7 shorter events, 0.1 us)
Async XLA Ops:
  3.8 1.6 %copy-start = (bf16[1,168,6144]{2,1,0:T(8,128)(2,1)S(1)}, bf16[1,168,6144]{2,1,0:T(8,128)(2,1)}, u32[]{:S(2)}) copy-start(bf16[1,168,6144]{2,1,0:T(8,128)(2,1)} %param.19) | copy-start | bytes 6193156
  5.4 0.8 %copy-start.1 = (bf16[2,6,2,1024]{3,2,1,0:T(2,128)(2,1)S(1)}, bf16[2,6,2,1024]{3,2,1,0:T(2,128)(2,1)}, u32[]{:S(2)}) copy-start(bf16[2,6,2,1024]{3,2,1,0:T(2,128)(2,1)} %param.11) | copy-start | bytes 147460
  6.2 0.7 copy-start.2

commit v2 on v1

v2 whole, which is shorter than its diff:
```python
import jax
import jax.numpy as jnp
from jax import lax
from jax.experimental import pallas as pl
from jax.experimental.pallas import tpu as pltpu
from jax.sharding import PartitionSpec as P

D = 6144
HEADS = 48
KV = 8
HD = 128
EXPERTS = 8
TOP = 4
CAP = 9
ROWS = 6
STEPS = 2
KEYS = 256
UNITS = 168
PART = 384
PACK = 80
EPS = 1e-05
BF = jnp.bfloat16
F32 = jnp.float32
MESH = pl.DeviceIdType.MESH
NT = (((1,), (1,)), ((), ()))
FAR_Z = (4, 3, 5, 2, 6, 1, 7)
FAR_PLANE = (10, 6, 9, 11, 14, 2, 8, 5, 7, 13, 15, 1, 3, 4, 12)
FAR_RING = (2, 1, 3)
MEMBERS = (2, 1, 3, 0)


def wrap(value, size):
    return lax.rem(value + size, size)


def iota(shape, dim):
    return lax.broadcasted_iota(jnp.int32, shape, dim)


def dot(a, b, dims=None):
    if dims is None:
        return jnp.dot(a, b, preferred_element_type=F32)
    return lax.dot_general(a, b, dims, preferred_element_type=F32)


def kernel(
    q_hbm, nkv_hbm, cache_hbm, res_hbm, wout_hbm, gain_hbm, routes_hbm, rw_hbm, win_hbm, wdn_hbm,
    out_ref,
    q_raw, nkv, res_raw, gain_ref, routes_raw, rw_raw, q_ref, res, choice,
    kv, wout, win, wdn,
    a_send, a_recv, stat, fcol, att, proj, b_send, b_recv,
    state, z_send, z_recv, xall, acc, vacc, hid,
    own, q_send, q_recv, g_send, g_recv, chip, m_send, m_recv, y_send, y_recv,
    in_sem, kv_sem, w_sem,
    a_ss, a_rs, b_ss, b_rs, z_ss, z_rs, x1_ss, x1_rs, x2_ss, x2_rs, xp_ss, xp_rs,
    q_ss, q_rs, g_ss, g_rs, m_ss, m_rs, y_ss, y_rs,
):
    b = lax.axis_index("expert")
    t = lax.axis_index("tensor")
    z, c = lax.div(b, 2), lax.rem(b, 2)
    y, x = lax.div(t, 4), lax.rem(t, 4)
    partner = 2 * z + 1 - c
    m = (1 - c) * x + c * y
    g = (1 - c) * y + c * x

    def place(core, group, member):
        return (1 - core) * (4 * group + member) + core * (4 * member + group)

    def plane_peer(i):
        return 4 * wrap(y + i // 4, 4) + wrap(x + i % 4, 4)

    def remote(src, dst, ss, rs, dev):
        return pltpu.make_async_remote_copy(
            src_ref=src, dst_ref=dst, send_sem=ss, recv_sem=rs, device_id=dev, device_id_type=MESH
        )

    inputs = [
        pltpu.make_async_copy(src, dst, in_sem.at[i])
        for i, (src, dst) in enumerate(
            [
                (q_hbm, q_raw), (nkv_hbm, nkv), (res_hbm, res_raw), (gain_hbm, gain_ref),
                (routes_hbm, routes_raw), (rw_hbm, rw_raw),
            ]
        )
    ]
    rows_in = [
        [
            pltpu.make_async_copy(cache_hbm.at[s, r], kv.at[s, r], kv_sem.at[s, r])
            for s in range(2)
        ]
        for r in range(ROWS)
    ]
    weights_in = [
        pltpu.make_async_copy(wout_hbm, wout, w_sem.at[0]),
        pltpu.make_async_copy(win_hbm, win, w_sem.at[1]),
        pltpu.make_async_copy(wdn_hbm, wdn, w_sem.at[2]),
    ]
    inputs[0].start()
    inputs[1].start()
    for pair in rows_in:
        for copy in pair:
            copy.start()
    for copy in inputs[2:]:
        copy.start()

    barrier = pltpu.get_barrier_semaphore()

    def greet(dev):
        pl.semaphore_signal(barrier, inc=1, device_id=dev, device_id_type=MESH)

    for d in FAR_Z:
        greet((2 * wrap(z + d, 8) + c, t))
    for i in FAR_PLANE:
        greet((b, plane_peer(i)))
    greet((partner, t))

    inputs[0].wait()
    nothing = jnp.zeros((2, HD), F32)
    for r in range(ROWS):
        both = q_raw[r].astype(F32)
        pieces = []
        for owner in range(16):
            for h in range(3):
                lo = HD * (3 * owner + h)
                pieces.append(both[:, lo : lo + HD])
            pieces.append(nothing)
        q_ref[r] = jnp.concatenate(pieces, axis=0).astype(BF)
    inputs[1].wait()

    row_id = iota((128, 16), 0)
    key_id = iota((128, 16), 1)
    fresh_ok = (
        (lax.div(row_id, 16) == lax.div(key_id, 2))
        & (lax.rem(key_id, 2) <= lax.rem(row_id, 2))
        & (jnp.broadcast_to(t, (128, 16)) == 0)
    )
    lane = iota((128, 128), 1)
    tallies = jnp.zeros((128, 128), F32)
    for pair in range(3):
        if pair == 2:
            weights_in[0].start()
        halves = []
        for r in (2 * pair, 2 * pair + 1):
            rows_in[r][0].wait()
            qr = q_ref[r]
            scores = jnp.concatenate(
                [dot(qr[16 * k : 16 * k + 16], kv[0, r, k], NT) for k in range(KV)], axis=0
            ) * (HD**-0.5)
            extra = dot(qr, nkv[0, r], NT) * (HD**-0.5)
            extra = jnp.where(fresh_ok, extra, -jnp.inf)
            top = jnp.maximum(
                jnp.max(scores, axis=1, keepdims=True), jnp.max(extra, axis=1, keepdims=True)
            )
            top = jnp.ceil(top * 0.25) * 4.0
            weights = jnp.exp(scores - top)
            extra = jnp.exp(extra - top)
            total = jnp.sum(weights, axis=1, keepdims=True) + jnp.sum(extra, axis=1, keepdims=True)
            low = weights.astype(BF)
            rows_in[r][1].wait()
            mixed = jnp.concatenate(
                [dot(low[16 * k : 16 * k + 16], kv[1, r, k]) for k in range(KV)], axis=0
            ) + dot(extra.astype(BF), nkv[1, r])
            tallies = jnp.where(lane == r, top, jnp.where(lane == 8 + r, total, tallies))
            halves.append(mixed.reshape(16, 8, 128))
        a_send[:, 16 * pair : 16 * pair + 16, :] = jnp.concatenate(halves, axis=1).astype(BF)
    table = jnp.transpose(tallies)[0:16, :].astype(BF)
    a_send[:, 48:64, :] = jnp.broadcast_to(table[None], (16, 16, 128))
    pl.semaphore_wait(barrier, 23)

    def a_copy(i):
        to = plane_peer(i)
        return remote(a_send.at[to], a_recv.at[t], a_ss.at[i], a_rs.at[i], (b, to))

    for i in FAR_PLANE:
        a_copy(i).start()
    a_recv[t] = a_send[t]
    weights_in[1].start()
    weights_in[2].start()

    for copy in inputs[2:]:
        copy.wait()
    choice[...] = jnp.zeros_like(choice)
    for s in range(STEPS):
        choice[4 * s : 4 * s + 4, 0:ROWS] = routes_raw[s].astype(F32) + 1.0
        choice[8 + 4 * s : 12 + 4 * s, 0:ROWS] = rw_raw[s]
    turned = jnp.transpose(choice[...])
    slot_lane = iota((16, 128), 1)
    token_row = iota((16, 128), 0)
    lane_expert = lax.div(slot_lane, 16).astype(F32) + 1.0
    chosen = jnp.zeros((16, 128), F32)
    factor = jnp.zeros((16, 128), F32)
    for k in range(TOP):
        named = jnp.concatenate([turned[0:8, k : k + 1], turned[0:8, 4 + k : 5 + k]], axis=0)
        amount = jnp.concatenate([turned[0:8, 8 + k : 9 + k], turned[0:8, 12 + k : 13 + k]], axis=0)
        hit = named == lane_expert
        chosen = jnp.where(hit, 1.0, chosen)
        factor = jnp.where(hit, amount, factor)
    below = (iota((16, 16), 1) < iota((16, 16), 0)).astype(BF)
    earlier = dot(below, chosen.astype(BF))
    here = (chosen > 0.5) & (earlier.astype(jnp.int32) == lax.rem(slot_lane, 16))
    dispatch = jnp.transpose(
        jnp.concatenate([jnp.where(here, 1.0, 0.0), jnp.zeros((112, 128), F32)], axis=0)
    )[:, 0:16].astype(BF)
    combine = jnp.where(here, factor, 0.0)
    combine_high = combine.astype(BF)
    combine_low = (combine - combine_high.astype(F32)).astype(BF)
    mine = pl.ds(pl.multiple_of(t * PART, 128), PART)
    res[...] = jnp.zeros_like(res)
    for r in range(ROWS):
        both = res_raw[r].astype(F32)
        res[r : r + 1, :] = both[0:1]
        res[8 + r : 9 + r, :] = both[1:2]
    res_sum = jnp.sum(res[...], axis=1, keepdims=True)
    res_mine = res[:, mine]
    gain_mine = gain_ref[:, mine]

    def slots(row, slot):
        rank = lax.rem(slot, 16)
        return jnp.where((row == CAP * lax.div(slot, 16) + rank) & (rank < CAP), 1.0, 0.0).astype(BF)

    packing = slots(iota((PACK, 128), 0), iota((PACK, 128), 1))
    unpacking = slots(iota((128, PACK), 1), iota((128, PACK), 0))
    acc[...] = jnp.zeros_like(acc)
    vacc[...] = jnp.zeros_like(vacc)
    att[...] = jnp.zeros_like(att)
    weights_in[0].wait()

    for i in reversed(FAR_PLANE):
        a_copy(i).wait_recv()

    stats = a_recv[:, 48:64, :].astype(F32)
    tops, totals = stats[:, 0:8], stats[:, 8:16]
    top = jnp.max(tops, axis=0, keepdims=True)
    scale = jnp.exp(tops - top)
    whole = jnp.sum(scale * totals, axis=0, keepdims=True)
    scale = scale / jnp.maximum(whole, 1e-30)
    fcol[...] = jnp.transpose(scale.reshape(128, 128))
    columns = fcol[pl.ds(pl.multiple_of(8 * t, 8), 8), :]
    for pair in range(3):
        both = a_recv[:, 16 * pair : 16 * pair + 16, :].astype(F32)
        for half in range(2):
            r = 2 * pair + half
            joined = jnp.zeros((8, 128), F32)
            for s in range(16):
                joined += both[s, 8 * half : 8 * half + 8] * columns[:, 8 * s + r : 8 * s + r + 1]
            for h in range(3):
                for s in range(STEPS):
                    att[8 * s + r : 8 * s + r + 1, 128 * h : 128 * h + 128] = joined[
                        2 * h + s : 2 * h + s + 1
                    ]

    attended = att[...].astype(BF)
    proj_sum = jnp.zeros((16, 1), F32)
    for s in range(16):
        part = dot(attended, wout[:, PART * s : PART * s + PART])
        proj[s] = part
        proj_sum = proj_sum + jnp.sum(part, axis=1, keepdims=True)
    diagonal = jnp.sum(jnp.where(token_row == slot_lane, proj_sum, 0.0), axis=0, keepdims=True)
    high = diagonal.astype(BF).astype(F32)
    low = diagonal - high
    head = jnp.where(token_row == 6, high, jnp.where(token_row == 7, low, 0.0))
    head = jnp.concatenate([head, jnp.zeros((16, PART - 128), F32)], axis=1)

    def b_copy(i):
        to = plane_peer(i)
        return remote(b_send.at[to], b_recv.at[t], b_ss.at[i], b_rs.at[i], (b, to))

    for i in FAR_PLANE:
        to = plane_peer(i)
        b_send[to] = (proj[to] + head).astype(BF)
        b_copy(i).start()
    b_recv[t] = (proj[t] + head).astype(BF)
    for i in reversed(FAR_PLANE):
        b_copy(i).wait_recv()

    summed = jnp.sum(b_recv[...].astype(F32), axis=0)
    spread = jnp.where(token_row == slot_lane, summed[6:7, 0:128] + summed[7:8, 0:128], 0.0)
    mean = (jnp.sum(spread, axis=1, keepdims=True) + res_sum) * (1.0 / D)
    real = lax.rem(iota((16, PART), 0), 8) < ROWS
    hidden = jnp.where(real, summed + res_mine, 0.0)
    state[...] = hidden
    scaled = jnp.where(real, (hidden - mean) * gain_mine, 0.0).astype(BF)

    z_send[...] = dot(dispatch, scaled).astype(BF).reshape(EXPERTS, 16, PART)

    def z_copy(d):
        to = wrap(z + d, 8)
        return remote(z_send.at[to], z_recv.at[z], z_ss.at[d], z_rs.at[d], (2 * to + c, t))

    for d in FAR_Z:
        z_copy(d).start()
    z_recv[z] = z_send[z]
    weights_in[1].wait()
    weights_in[2].wait()
    for d in reversed(FAR_Z):
        z_copy(d).wait_recv()
    xall[c, t] = dot(packing, z_recv[...].reshape(128, PART)).astype(BF)

    def x1_copy(j):
        return remote(
            xall.at[c, t], xall.at[c, t], x1_ss.at[j], x1_rs.at[j], (b, place(c, g, wrap(m + j, 4)))
        )

    def x2_copy(j, d):
        s = place(c, g, wrap(m - j, 4))
        n = 4 * j + d
        return remote(
            xall.at[c, s], xall.at[c, s], x2_ss.at[n], x2_rs.at[n], (b, place(c, wrap(g + d, 4), m))
        )

    def xp_copy(j, d):
        s = place(c, wrap(g - d, 4), wrap(m - j, 4))
        n = 4 * j + d
        return remote(xall.at[c, s], xall.at[c, s], xp_ss.at[n], xp_rs.at[n], (partner, t))

    def multiply(core, side, found):
        rows = jnp.concatenate([xall[core, s] for s in found], axis=1)
        cols = [pl.ds(pl.multiple_of(s * PART, 128), PART) for s in found]
        for u in range(2):
            units = jnp.concatenate([win[u, :, col] for col in cols], axis=1)
            acc[side, u] += dot(rows, units, NT)
        squares = vacc[side]
        for s, col in zip(found, cols):
            plain = xall[core, s].astype(F32) * (1.0 / gain_ref[:, col])
            plain = plain * plain
            squares += plain[:, 0:128] + plain[:, 128:256] + plain[:, 256:384]
        vacc[side] = squares

    def own_part(j):
        for d in FAR_RING:
            x2_copy(j, d).wait_recv()
            xp_copy(j, d).start()

    def own_multiply(j):
        multiply(c, 0, [place(c, wrap(g - d, 4), wrap(m - j, 4)) for d in range(4)])

    def partner_multiply(j):
        for d in range(4):
            xp_copy(j, d).wait_recv()
        multiply(1 - c, 1, [place(1 - c, wrap(m - d, 4), wrap(g - j, 4)) for d in range(4)])

    for j in FAR_RING:
        x1_copy(j).start()
    for d in FAR_RING:
        x2_copy(0, d).start()
    xp_copy(0, 0).start()
    for j in (1, 3, 2):
        x1_copy(j).wait_recv()
        for d in FAR_RING:
            x2_copy(j, d).start()
        xp_copy(j, 0).start()
    own_part(0)
    own_multiply(0)
    own_part(1)
    own_multiply(1)
    partner_multiply(0)
    own_part(3)
    own_multiply(3)
    partner_multiply(1)
    own_part(2)
    partner_multiply(3)
    own_multiply(2)
    partner_multiply(2)

    for side in range(2):
        inverse = lax.rsqrt(jnp.sum(vacc[side], axis=1, keepdims=True) * (1.0 / D) + EPS)
        gate, up = acc[side, 0] * inverse, acc[side, 1] * inverse
        hid[PACK * side : PACK * side + PACK] = (gate / (1.0 + jnp.exp(-gate)) * up).astype(BF)

    def q_copy(n):
        part = pl.ds(4 * n, 4)
        return remote(q_send.at[part], q_recv.at[part], q_ss.at[n], q_rs.at[n], (partner, t))

    for n in range(4):
        slab = dot(hid[...], wdn[:, 4 * PART * n : 4 * PART * n + 4 * PART])
        for i in range(4):
            q_send[4 * n + i] = slab[PACK:, PART * i : PART * i + PART].astype(BF)
        q_copy(n).start()
        for i in range(4):
            own[4 * n + i] = slab[:PACK, PART * i : PART * i + PART]

    def g_copy(j, d):
        n = 3 * j + d - 1
        return remote(
            g_send.at[n], g_recv.at[n], g_ss.at[n], g_rs.at[n], (b, place(c, wrap(g + d, 4), m))
        )

    def m_copy(j):
        return remote(
            m_send.at[j], m_recv.at[j], m_ss.at[j], m_rs.at[j], (b, place(c, g, wrap(m + j, 4)))
        )

    for n in range(4):
        q_copy(n).wait_recv()
    for j in MEMBERS:
        for d in FAR_RING:
            s = place(c, wrap(g + d, 4), wrap(m + j, 4))
            g_send[3 * j + d - 1] = (own[s] + q_recv[s].astype(F32)).astype(BF)
            g_copy(j, d).start()
        s = place(c, g, wrap(m + j, 4))
        chip[j] = own[s] + q_recv[s].astype(F32)

    final = None
    for j in MEMBERS:
        whole = chip[j]
        for d in FAR_RING:
            g_copy(j, d).wait_recv()
            whole = whole + g_recv[3 * j + d - 1].astype(F32)
        if j:
            m_send[j] = whole.astype(BF)
            m_copy(j).start()
        else:
            final = whole
    for j in (1, 3, 2):
        m_copy(j).wait_recv()
        final = final + m_recv[j].astype(F32)

    y_send[...] = dot(unpacking, final.astype(BF)).astype(BF).reshape(EXPERTS, 16, PART)

    def y_copy(d):
        to = wrap(z + d, 8)
        return remote(y_send.at[to], y_recv.at[z], y_ss.at[d], y_rs.at[d], (2 * to + c, t))

    for d in FAR_Z:
        y_copy(d).start()
    y_recv[z] = y_send[z]

    for i in FAR_PLANE:
        a_copy(i).wait_send()
        b_copy(i).wait_send()
    for d in FAR_Z:
        z_copy(d).wait_send()
    for j in FAR_RING:
        x1_copy(j).wait_send()
        m_copy(j).wait_send()
    for j in range(4):
        q_copy(j).wait_send()
        for d in range(4):
            xp_copy(j, d).wait_send()
        for d in FAR_RING:
            x2_copy(j, d).wait_send()
            g_copy(j, d).wait_send()

    for d in reversed(FAR_Z):
        y_copy(d).wait_recv()
    returned = y_recv[...].reshape(128, PART)
    mix = dot(combine_high, returned) + dot(combine_low, returned)
    mixed = state[...] + mix
    for r in range(ROWS):
        out_ref[r] = jnp.concatenate([mixed[r : r + 1], mixed[8 + r : 9 + r]], axis=0).astype(BF)
    for d in FAR_Z:
        y_copy(d).wait_send()


def body(queries, new_kv, cache, residual, w_out, norm_gain, routes, route_weight, w_in, w_down):
    fresh = new_kv.reshape(2, ROWS, STEPS, KV, HD).transpose(0, 1, 3, 2, 4)
    fresh = fresh.reshape(2, ROWS, 16, HD)
    w_in_t = w_in.transpose(0, 2, 3, 1).reshape(2, UNITS, D)
    w_down = w_down.reshape(UNITS, D)
    gain = norm_gain.reshape(1, D)
    chosen = routes.transpose(1, 2, 0)
    factors = route_weight.transpose(1, 2, 0)
    hbm = pl.BlockSpec(memory_space=pltpu.HBM)
    dma = pltpu.SemaphoreType.DMA
    vmem = pltpu.VMEM
    return pl.pallas_call(
        kernel,
        out_shape=jax.ShapeDtypeStruct((ROWS, STEPS, PART), BF),
        in_specs=[hbm] * 10,
        out_specs=pl.BlockSpec(memory_space=pltpu.VMEM),
        scratch_shapes=[
            vmem((ROWS, STEPS, D), BF),
            vmem((2, ROWS, 16, HD), BF),
            vmem((ROWS, STEPS, D), BF),
            vmem((1, D), F32),
            vmem((STEPS, TOP, ROWS), jnp.int32),
            vmem((STEPS, TOP, ROWS), F32),
            vmem((ROWS, 128, HD), BF),
            vmem((16, D), F32),
            vmem((128, 128), F32),
            vmem((2, ROWS, KV, KEYS, HD), BF),
            vmem((PART, D), BF),
            vmem((2, UNITS, D), BF),
            vmem((UNITS, D), BF),
            vmem((16, 64, 128), BF),
            vmem((16, 64, 128), BF),
            vmem((128, 128), F32),
            vmem((128, 128), F32),
            vmem((16, PART), F32),
            vmem((16, 16, PART), F32),
            vmem((16, 16, PART), BF),
            vmem((16, 16, PART), BF),
            vmem((16, PART), F32),
            vmem((EXPERTS, 16, PART), BF),
            vmem((EXPERTS, 16, PART), BF),
            vmem((2, 16, PACK, PART), BF),
            vmem((2, 2, PACK, UNITS), F32),
            vmem((2, PACK, 128), F32),
            vmem((2 * PACK, UNITS), BF),
            vmem((16, PACK, PART), F32),
            vmem((16, PACK, PART), BF),
            vmem((16, PACK, PART), BF),
            vmem((12, PACK, PART), BF),
            vmem((12, PACK, PART), BF),
            vmem((4, PACK, PART), F32),
            vmem((4, PACK, PART), BF),
            vmem((4, PACK, PART), BF),
            vmem((EXPERTS, 16, PART), BF),
            vmem((EXPERTS, 16, PART), BF),
            dma((6,)),
            dma((2, ROWS)),
            dma((3,)),
            dma((16,)), dma((16,)),
            dma((16,)), dma((16,)),
            dma((8,)), dma((8,)),
            dma((4,)), dma((4,)),
            dma((16,)), dma((16,)),
            dma((16,)), dma((16,)),
            dma((4,)), dma((4,)),
            dma((12,)), dma((12,)),
            dma((4,)), dma((4,)),
            dma((8,)), dma((8,)),
        ],
        compiler_params=pltpu.CompilerParams(
            collective_id=0, has_side_effects=True, vmem_limit_bytes=56 * 1024 * 1024
        ),
        name="layer",
    )(queries, fresh, cache, residual, w_out, gain, chosen, factors, w_in_t, w_down)


def solution(mesh):
    return jax.shard_map(
        body,
        mesh=mesh,
        in_specs=(
            P("expert", None, None),
            P(None, "expert", None, None),
            P(None, "expert", None, "tensor", None),
            P("expert", None, None),
            P("tensor", None),
            P(),
            P("expert", None, None),
            P("expert", None, None),
            P("expert", None, None, "tensor"),
            P("expert", "tensor", None),
        ),
        out_specs=P("expert", None, "tensor"),
        check_vma=False,
    )
```

time: 75.1 us -> 65.3 us (0.87); the launches traced: 74 us -> 65.1 us
  local copies, waits for them, and re-layouts: 7.48 us -> 1.31 us
  Pallas kernels: 66.4 us -> 63.8 us
    unnamed x9 -> x1, local copies, waits for them, and re-layouts: 4.72 us -> 1.31 us
    reshape x6 -> x0, local copies, waits for them, and re-layouts: 2.7 us -> none  [the longest x1 1.04 us: body(): heads = queries.reshape(ROWS, STEPS, 16, 3, HD).transpose(0, 2, 3, 1, 4)]
    pallas_call x1, Pallas kernels: 66.4 us -> 63.8 us  [body(): pl.pallas_call(kernel, out_shape=jax.ShapeDtypeStruct((ROWS, STEPS, PART)...]
where the time goes in v2:
time: 65.3 us; the launch traced here: 65.1 us
  Pallas kernels  63.8 us (98%)
  local copies, waits for them, and re-layouts  1.31 us (2%)
    pallas_call x1, Pallas kernels, body(): pl.pallas_call(kernel, out_shape=jax.ShapeDtypeStruct((ROWS, STEPS, PART)...  63.8 us

profile of v2, /device:TPU:6, one launch (start us, length us, event | category | flops | bytes accessed | tf_op | source)
XLA Modules:
  0.0 65.1 jit_solution(13129244528247245564)
XLA Ops:
  0.0 63.8 %layer.1 = bf16[6,2,384]{2,1,0:T(2,128)(2,1)} custom-call(bf16[6,2,6144]{2,1,0:T(2,128)(2,1)} %q_hbm.1, bf16[2,6,16,128]{3,2,1,0:T(8,128)(2,1)} %bitcast.14, bf16[2,6,8,256,128]{4,3,2,1,0:T(8,128)(2,1)} %cache_hbm.1, bf16[6,2,6144]{2,1,0:T(2,128)(2,1)} %res_hbm.1, bf16[384,6144]{1,0:T(8,128)(2,1)} %wout_hbm.1, f32[1,6144]{1,0:T(1,128)} %bitcast.15, ...), custom_call_target="tpu_custom_call" | custom-call | tf_op jit(solution)/shard_map/layer/pallas_call | solution.py:466
  63.8 1.3 %copy.13 = bf16[6,2,384]{2,1,0:T(2,128)(2,1)} copy(bf16[6,2,384]{2,1,0:T(2,128)(2,1)} %layer.1) | data formatting | bytes 18432

commit v3 on v2

--- a/solution.py
+++ b/solution.py
@@ -26,6 +26,9 @@
 FAR_Z = (4, 3, 5, 2, 6, 1, 7)
 FAR_PLANE = (10, 6, 9, 11, 14, 2, 8, 5, 7, 13, 15, 1, 3, 4, 12)
 FAR_RING = (2, 1, 3)
+ORDER = (0, 1, 7, 2, 6, 3, 5, 4)
+NEAR = 5
+GROUPS = ((0, 48), (48, 32))
 MEMBERS = (2, 1, 3, 0)
 
 
@@ -46,11 +49,11 @@
 def kernel(
     q_hbm, nkv_hbm, cache_hbm, res_hbm, wout_hbm, gain_hbm, routes_hbm, rw_hbm, win_hbm, wdn_hbm,
     out_ref,
-    q_raw, nkv, res_raw, gain_ref, routes_raw, rw_raw, q_ref, res, choice,
+    q_raw, nkv, res_raw, gain_ref, routes_raw, rw_raw, q_ref, res, choice, ordered,
     kv, wout, win, wdn,
     a_send, a_recv, stat, fcol, att, proj, b_send, b_recv,
     state, z_send, z_recv, xall, acc, vacc, hid,
-    own, q_send, q_recv, g_send, g_recv, chip, m_send, m_recv, y_send, y_recv,
+    own, q_send, q_recv, g_send, g_recv, m_send, m_recv, y_send, y_recv,
     in_sem, kv_sem, w_sem,
     a_ss, a_rs, b_ss, b_rs, z_ss, z_rs, x1_ss, x1_rs, x2_ss, x2_rs, xp_ss, xp_rs,
     q_ss, q_rs, g_ss, g_rs, m_ss, m_rs, y_ss, y_rs,
@@ -97,11 +100,9 @@
     ]
     inputs[0].start()
     inputs[1].start()
-    for pair in rows_in:
+    for pair in rows_in[:3]:
         for copy in pair:
             copy.start()
-    for copy in inputs[2:]:
-        copy.start()
 
     barrier = pltpu.get_barrier_semaphore()
 
@@ -137,11 +138,15 @@
     lane = iota((128, 128), 1)
     tallies = jnp.zeros((128, 128), F32)
     for pair in range(3):
-        if pair == 2:
-            weights_in[0].start()
         halves = []
         for r in (2 * pair, 2 * pair + 1):
             rows_in[r][0].wait()
+            if r + 3 < ROWS:
+                for copy in rows_in[r + 3]:
+                    copy.start()
+            if r == 3:
+                for copy in inputs[2:] + weights_in[:1]:
+                    copy.start()
             qr = q_ref[r]
             scores = jnp.concatenate(
                 [dot(qr[16 * k : 16 * k + 16], kv[0, r, k], NT) for k in range(KV)], axis=0
@@ -201,7 +206,13 @@
     dispatch = jnp.transpose(
         jnp.concatenate([jnp.where(here, 1.0, 0.0), jnp.zeros((112, 128), F32)], axis=0)
     )[:, 0:16].astype(BF)
+    ordered[...] = jnp.zeros_like(ordered)
     combine = jnp.where(here, factor, 0.0)
+    for r in range(ROWS):
+        for s in range(STEPS):
+            ordered[2 * r + s : 2 * r + s + 1, :] = combine[8 * s + r : 8 * s + r + 1]
+    combine = ordered[...]
+    state[...] = jnp.zeros_like(state)
     combine_high = combine.astype(BF)
     combine_low = (combine - combine_high.astype(F32)).astype(BF)
     mine = pl.ds(pl.multiple_of(t * PART, 128), PART)
@@ -218,8 +229,9 @@
         rank = lax.rem(slot, 16)
         return jnp.where((row == CAP * lax.div(slot, 16) + rank) & (rank < CAP), 1.0, 0.0).astype(BF)
 
-    packing = slots(iota((PACK, 128), 0), iota((PACK, 128), 1))
-    unpacking = slots(iota((128, PACK), 1), iota((128, PACK), 0))
+    spans = (16 * NEAR, 16 * (EXPERTS - NEAR))
+    packing = [slots(iota((n, w), 0), iota((n, w), 1)) for (_, n), w in zip(GROUPS, spans)]
+    unpacking = [slots(iota((w, n), 1), iota((w, n), 0)) for (_, n), w in zip(GROUPS, spans)]
     acc[...] = jnp.zeros_like(acc)
     vacc[...] = jnp.zeros_like(vacc)
     att[...] = jnp.zeros_like(att)
@@ -278,178 +290,210 @@
     mean = (jnp.sum(spread, axis=1, keepdims=True) + res_sum) * (1.0 / D)
     real = lax.rem(iota((16, PART), 0), 8) < ROWS
     hidden = jnp.where(real, summed + res_mine, 0.0)
-    state[...] = hidden
     scaled = jnp.where(real, (hidden - mean) * gain_mine, 0.0).astype(BF)
 
     z_send[...] = dot(dispatch, scaled).astype(BF).reshape(EXPERTS, 16, PART)
 
-    def z_copy(d):
-        to = wrap(z + d, 8)
-        return remote(z_send.at[to], z_recv.at[z], z_ss.at[d], z_rs.at[d], (2 * to + c, t))
-
-    for d in FAR_Z:
-        z_copy(d).start()
-    z_recv[z] = z_send[z]
-    weights_in[1].wait()
-    weights_in[2].wait()
-    for d in reversed(FAR_Z):
-        z_copy(d).wait_recv()
-    xall[c, t] = dot(packing, z_recv[...].reshape(128, PART)).astype(BF)
-
-    def x1_copy(j):
-        return remote(
-            xall.at[c, t], xall.at[c, t], x1_ss.at[j], x1_rs.at[j], (b, place(c, g, wrap(m + j, 4)))
-        )
-
-    def x2_copy(j, d):
-        s = place(c, g, wrap(m - j, 4))
-        n = 4 * j + d
-        return remote(
-            xall.at[c, s], xall.at[c, s], x2_ss.at[n], x2_rs.at[n], (b, place(c, wrap(g + d, 4), m))
-        )
+    def z_copy(p):
+        to = wrap(z + ORDER[p], 8)
+        return remote(z_send.at[to], z_recv.at[p], z_ss.at[p], z_rs.at[p], (2 * to + c, t))
+
+    for p in range(7, 0, -1):
+        z_copy(p).start()
+    z_recv[0] = z_send[z]
+
+    def rows_of(s, group):
+        lo, n = GROUPS[group]
+        return xall.at[c, s, pl.ds(lo, n)]
+
+    def x1_copy(j, group):
+        part = rows_of(t, group)
+        n = 2 * j + group
+        return remote(part, part, x1_ss.at[n], x1_rs.at[n], (b, place(c, g, wrap(m + j, 4))))
+
+    def x2_copy(j, d, group):
+        part = rows_of(place(c, g, wrap(m - j, 4)), group)
+        n = 8 * j + 2 * d + group
+        return remote(part, part, x2_ss.at[n], x2_rs.at[n], (b, place(c, wrap(g + d, 4), m)))
 
     def xp_copy(j, d):
         s = place(c, wrap(g - d, 4), wrap(m - j, 4))
         n = 4 * j + d
         return remote(xall.at[c, s], xall.at[c, s], xp_ss.at[n], xp_rs.at[n], (partner, t))
 
-    def multiply(core, side, found):
-        rows = jnp.concatenate([xall[core, s] for s in found], axis=1)
+    def multiply(offsets):
+        found = [4 * wrap(y - i, 4) + wrap(x - j, 4) for i, j in offsets]
         cols = [pl.ds(pl.multiple_of(s * PART, 128), PART) for s in found]
+        both = [jnp.concatenate([xall[c, s], xall[1 - c, s]], axis=0) for s in found]
+        rows = jnp.concatenate(both, axis=1)
         for u in range(2):
             units = jnp.concatenate([win[u, :, col] for col in cols], axis=1)
-            acc[side, u] += dot(rows, units, NT)
-        squares = vacc[side]
-        for s, col in zip(found, cols):
-            plain = xall[core, s].astype(F32) * (1.0 / gain_ref[:, col])
+            acc[u] += dot(rows, units, NT)
+        squares = vacc[...]
+        for part, col in zip(both, cols):
+            plain = part.astype(F32) * (1.0 / gain_ref[:, col])
             plain = plain * plain
             squares += plain[:, 0:128] + plain[:, 128:256] + plain[:, 256:384]
-        vacc[side] = squares
-
-    def own_part(j):
+        vacc[...] = squares
+
+    for group in range(2):
+        span = range(1, NEAR) if group == 0 else range(NEAR, EXPERTS)
+        for p in span:
+            z_copy(p).wait_recv()
+        blocks = z_recv[0:NEAR] if group == 0 else z_recv[NEAR:EXPERTS]
+        lo, n = GROUPS[group]
+        xall[c, t, lo : lo + n] = dot(
+            packing[group], blocks.reshape(spans[group], PART)
+        ).astype(BF)
+        for j in FAR_RING:
+            x1_copy(j, group).start()
         for d in FAR_RING:
-            x2_copy(j, d).wait_recv()
+            x2_copy(0, d, group).start()
+    xp_copy(0, 0).start()
+    for r in range(ROWS):
+        for s in range(STEPS):
+            state[2 * r + s : 2 * r + s + 1, :] = hidden[8 * s + r : 8 * s + r + 1]
+    weights_in[1].wait()
+    weights_in[2].wait()
+    for group in range(2):
+        for j in (1, 3, 2):
+            x1_copy(j, group).wait_recv()
+            for d in FAR_RING:
+                x2_copy(j, d, group).start()
+            if group:
+                xp_copy(j, 0).start()
+    for d in FAR_RING:
+        for group in range(2):
+            x2_copy(0, d, group).wait_recv()
+        xp_copy(0, d).start()
+    for n in range(4):
+        xp_copy(n, 0).wait_recv()
+    for d in FAR_RING:
+        xp_copy(0, d).wait_recv()
+    multiply([(0, 0), (0, 1), (0, 2), (0, 3), (1, 0), (2, 0), (3, 0)])
+    for j in (1, 3, 2):
+        for d in FAR_RING:
+            for group in range(2):
+                x2_copy(j, d, group).wait_recv()
             xp_copy(j, d).start()
-
-    def own_multiply(j):
-        multiply(c, 0, [place(c, wrap(g - d, 4), wrap(m - j, 4)) for d in range(4)])
-
-    def partner_multiply(j):
-        for d in range(4):
+    for j in (1, 3, 2):
+        for d in FAR_RING:
             xp_copy(j, d).wait_recv()
-        multiply(1 - c, 1, [place(1 - c, wrap(m - d, 4), wrap(g - j, 4)) for d in range(4)])
-
-    for j in FAR_RING:
-        x1_copy(j).start()
-    for d in FAR_RING:
-        x2_copy(0, d).start()
-    xp_copy(0, 0).start()
-    for j in (1, 3, 2):
-        x1_copy(j).wait_recv()
-        for d in FAR_RING:
-            x2_copy(j, d).start()
-        xp_copy(j, 0).start()
-    own_part(0)
-    own_multiply(0)
-    own_part(1)
-    own_multiply(1)
-    partner_multiply(0)
-    own_part(3)
-    own_multiply(3)
-    partner_multiply(1)
-    own_part(2)
-    partner_multiply(3)
-    own_multiply(2)
-    partner_multiply(2)
-
-    for side in range(2):
-        inverse = lax.rsqrt(jnp.sum(vacc[side], axis=1, keepdims=True) * (1.0 / D) + EPS)
-        gate, up = acc[side, 0] * inverse, acc[side, 1] * inverse
-        hid[PACK * side : PACK * side + PACK] = (gate / (1.0 + jnp.exp(-gate)) * up).astype(BF)
-
-    def q_copy(n):
-        part = pl.ds(4 * n, 4)
-        return remote(q_send.at[part], q_recv.at[part], q_ss.at[n], q_rs.at[n], (partner, t))
-
-    for n in range(4):
-        slab = dot(hid[...], wdn[:, 4 * PART * n : 4 * PART * n + 4 * PART])
-        for i in range(4):
-            q_send[4 * n + i] = slab[PACK:, PART * i : PART * i + PART].astype(BF)
-        q_copy(n).start()
-        for i in range(4):
-            own[4 * n + i] = slab[:PACK, PART * i : PART * i + PART]
-
-    def g_copy(j, d):
+    multiply([(i, j) for i in (1, 2, 3) for j in (1, 2, 3)])
+
+    inverse = lax.rsqrt(jnp.sum(vacc[...], axis=1, keepdims=True) * (1.0 / D) + EPS)
+    gate, up = acc[0] * inverse, acc[1] * inverse
+    hid[...] = (gate / (1.0 + jnp.exp(-gate)) * up).astype(BF)
+
+    def tiles(lo, found):
+        cols = [wdn[:, pl.ds(pl.multiple_of(s * PART, 128), PART)] for s in found]
+        slab = dot(hid[lo : lo + PACK], jnp.concatenate(cols, axis=1))
+        return [slab[:, PART * i : PART * i + PART] for i in range(4)]
+
+    def q_copy(j):
+        part = pl.ds(4 * j, 4)
+        return remote(q_send.at[part], q_recv.at[part], q_ss.at[j], q_rs.at[j], (partner, t))
+
+    def g_copy(j, d, group):
         n = 3 * j + d - 1
+        k = 2 * n + group
+        lo, rows = GROUPS[group]
+        part = pl.ds(lo, rows)
         return remote(
-            g_send.at[n], g_recv.at[n], g_ss.at[n], g_rs.at[n], (b, place(c, wrap(g + d, 4), m))
+            g_send.at[n, part], g_recv.at[n, part], g_ss.at[k], g_rs.at[k],
+            (b, place(c, wrap(g + d, 4), m)),
         )
 
-    def m_copy(j):
+    def m_copy(j, group):
+        k = 2 * j + group
+        lo, rows = GROUPS[group]
+        part = pl.ds(lo, rows)
         return remote(
-            m_send.at[j], m_recv.at[j], m_ss.at[j], m_rs.at[j], (b, place(c, g, wrap(m + j, 4)))
+            m_send.at[j, part], m_recv.at[j, part], m_ss.at[k], m_rs.at[k],
+            (b, place(c, g, wrap(m + j, 4))),
         )
 
-    for n in range(4):
-        q_copy(n).wait_recv()
+    def y_copy(p):
+        to = wrap(z - ORDER[p], 8)
+        return remote(y_send.at[p], y_recv.at[z], y_ss.at[p], y_rs.at[p], (2 * to + c, t))
+
     for j in MEMBERS:
-        for d in FAR_RING:
-            s = place(c, wrap(g + d, 4), wrap(m + j, 4))
-            g_send[3 * j + d - 1] = (own[s] + q_recv[s].astype(F32)).astype(BF)
-            g_copy(j, d).start()
-        s = place(c, g, wrap(m + j, 4))
-        chip[j] = own[s] + q_recv[s].astype(F32)
-
-    final = None
-    for j in MEMBERS:
-        whole = chip[j]
-        for d in FAR_RING:
-            g_copy(j, d).wait_recv()
-            whole = whole + g_recv[3 * j + d - 1].astype(F32)
-        if j:
-            m_send[j] = whole.astype(BF)
-            m_copy(j).start()
+        found = [place(1 - c, wrap(m + d, 4), wrap(g + j, 4)) for d in range(4)]
+        for d, tile in enumerate(tiles(PACK, found)):
+            q_send[4 * j + d] = tile.astype(BF)
+        q_copy(j).start()
+        found = [place(c, wrap(g + d, 4), wrap(m + j, 4)) for d in range(4)]
+        for d, tile in enumerate(tiles(0, found)):
+            own[4 * j + d] = tile
+
+    for group in (1, 0):
+        lo, n = GROUPS[group]
+        for j in MEMBERS:
+            if group:
+                q_copy(j).wait_recv()
+            for d in FAR_RING:
+                k = 4 * j + d
+                g_send[3 * j + d - 1, lo : lo + n] = (
+                    own[k, lo : lo + n] + q_recv[k, lo : lo + n].astype(F32)
+                ).astype(BF)
+                g_copy(j, d, group).start()
+
+    finals = [None, None]
+    for group in (1, 0):
+        lo, n = GROUPS[group]
+        for j in MEMBERS:
+            whole = own[4 * j, lo : lo + n] + q_recv[4 * j, lo : lo + n].astype(F32)
+            for d in FAR_RING:
+                g_copy(j, d, group).wait_recv()
+                whole = whole + g_recv[3 * j + d - 1, lo : lo + n].astype(F32)
+            if j:
+                m_send[j, lo : lo + n] = whole.astype(BF)
+                m_copy(j, group).start()
+            else:
+                finals[group] = whole
+
+    for group in (1, 0):
+        lo, n = GROUPS[group]
+        final = finals[group]
+        for j in (1, 3, 2):
+            m_copy(j, group).wait_recv()
+            final = final + m_recv[j, lo : lo + n].astype(F32)
+        back = dot(unpacking[group], final.astype(BF)).astype(BF)
+        if group:
+            y_send[NEAR:EXPERTS] = back.reshape(EXPERTS - NEAR, 16, PART)
+            for p in (7, 6, 5):
+                y_copy(p).start()
         else:
-            final = whole
-    for j in (1, 3, 2):
-        m_copy(j).wait_recv()
-        final = final + m_recv[j].astype(F32)
-
-    y_send[...] = dot(unpacking, final.astype(BF)).astype(BF).reshape(EXPERTS, 16, PART)
-
-    def y_copy(d):
-        to = wrap(z + d, 8)
-        return remote(y_send.at[to], y_recv.at[z], y_ss.at[d], y_rs.at[d], (2 * to + c, t))
-
-    for d in FAR_Z:
-        y_copy(d).start()
-    y_recv[z] = y_send[z]
+            y_send[0:NEAR] = back.reshape(NEAR, 16, PART)
+            for p in (4, 3, 2, 1):
+                y_copy(p).start()
+            y_recv[z] = y_send[0]
 
     for i in FAR_PLANE:
         a_copy(i).wait_send()
         b_copy(i).wait_send()
-    for d in FAR_Z:
-        z_copy(d).wait_send()
-    for j in FAR_RING:
-        x1_copy(j).wait_send()
-        m_copy(j).wait_send()
+    for p in range(1, 8):
+        z_copy(p).wait_send()
     for j in range(4):
         q_copy(j).wait_send()
         for d in range(4):
             xp_copy(j, d).wait_send()
-        for d in FAR_RING:
-            x2_copy(j, d).wait_send()
-            g_copy(j, d).wait_send()
-
-    for d in reversed(FAR_Z):
-        y_copy(d).wait_recv()
+    for group in range(2):
+        for j in FAR_RING:
+            x1_copy(j, group).wait_send()
+            m_copy(j, group).wait_send()
+        for j in range(4):
+            for d in FAR_RING:
+                x2_copy(j, d, group).wait_send()
+                g_copy(j, d, group).wait_send()
+
+    for p in range(1, 8):
+        y_copy(p).wait_recv()
     returned = y_recv[...].reshape(128, PART)
     mix = dot(combine_high, returned) + dot(combine_low, returned)
-    mixed = state[...] + mix
-    for r in range(ROWS):
-        out_ref[r] = jnp.concatenate([mixed[r : r + 1], mixed[8 + r : 9 + r]], axis=0).astype(BF)
-    for d in FAR_Z:
-        y_copy(d).wait_send()
+    out_ref[...] = (state[...] + mix).astype(BF)
+    for p in range(1, 8):
+        y_copy(p).wait_send()
 
 
 def body(queries, new_kv, cache, residual, w_out, norm_gain, routes, route_weight, w_in, w_down):
@@ -463,9 +507,9 @@
     hbm = pl.BlockSpec(memory_space=pltpu.HBM)
     dma = pltpu.SemaphoreType.DMA
     vmem = pltpu.VMEM
-    return pl.pallas_call(
+    out = pl.pallas_call(
         kernel,
-        out_shape=jax.ShapeDtypeStruct((ROWS, STEPS, PART), BF),
+        out_shape=jax.ShapeDtypeStruct((16, PART), BF),
         in_specs=[hbm] * 10,
         out_specs=pl.BlockSpec(memory_space=pltpu.VMEM),
         scratch_shapes=[
@@ -478,6 +522,7 @@
             vmem((ROWS, 128, HD), BF),
             vmem((16, D), F32),
             vmem((128, 128), F32),
+            vmem((16, 128), F32),
             vmem((2, ROWS, KV, KEYS, HD), BF),
             vmem((PART, D), BF),
             vmem((2, UNITS, D), BF),
@@ -494,15 +539,14 @@
             vmem((EXPERTS, 16, PART), BF),
             vmem((EXPERTS, 16, PART), BF),
             vmem((2, 16, PACK, PART), BF),
-            vmem((2, 2, PACK, UNITS), F32),
-            vmem((2, PACK, 128), F32),
+            vmem((2, 2 * PACK, UNITS), F32),
+            vmem((2 * PACK, 128), F32),
             vmem((2 * PACK, UNITS), BF),
             vmem((16, PACK, PART), F32),
             vmem((16, PACK, PART), BF),
             vmem((16, PACK, PART), BF),
             vmem((12, PACK, PART), BF),
             vmem((12, PACK, PART), BF),
-            vmem((4, PACK, PART), F32),
             vmem((4, PACK, PART), BF),
             vmem((4, PACK, PART), BF),
             vmem((EXPERTS, 16, PART), BF),
@@ -513,12 +557,12 @@
             dma((16,)), dma((16,)),
             dma((16,)), dma((16,)),
             dma((8,)), dma((8,)),
-            dma((4,)), dma((4,)),
-            dma((16,)), dma((16,)),
+            dma((8,)), dma((8,)),
+            dma((32,)), dma((32,)),
             dma((16,)), dma((16,)),
             dma((4,)), dma((4,)),
-            dma((12,)), dma((12,)),
-            dma((4,)), dma((4,)),
+            dma((24,)), dma((24,)),
+            dma((8,)), dma((8,)),
             dma((8,)), dma((8,)),
         ],
         compiler_params=pltpu.CompilerParams(
@@ -526,6 +570,7 @@
         ),
         name="layer",
     )(queries, fresh, cache, residual, w_out, gain, chosen, factors, w_in_t, w_down)
+    return out[:12].reshape(ROWS, STEPS, PART)
 
 
 def solution(mesh):

time: 65.3 us -> 63.5 us (0.972)
  Pallas kernels: 63.8 us -> 62 us
    pallas_call x1, Pallas kernels: 63.8 us -> 62 us  [body(): pl.pallas_call(kernel, out_shape=jax.ShapeDtypeStruct((16, PART), BF), in...]
    reshape x0 -> x1, local copies, waits for them, and re-layouts: none -> 1.32 us  [body(): return out[:12].reshape(ROWS, STEPS, PART)]
    unnamed x1 -> x0, local copies, waits for them, and re-layouts: 1.31 us -> none
where the time goes in v3:
time: 63.5 us; the launch traced here: 63.3 us
  Pallas kernels  62 us (98%)
  local copies, waits for them, and re-layouts  1.32 us (2%)
    pallas_call x1, Pallas kernels, body(): pl.pallas_call(kernel, out_shape=jax.ShapeDtypeStruct((16, PART), BF), in...  62 us
    reshape x1, local copies, waits for them, and re-layouts, body(): return out[:12].reshape(ROWS, STEPS, PART)  1.32 us

profile of v3, /device:TPU:6, one launch (start us, length us, event | category | flops | bytes accessed | tf_op | source)
XLA Modules:
  0.0 63.3 jit_solution(329469718899107059)
XLA Ops:
  0.0 62.0 %layer.1 = bf16[16,384]{1,0:T(8,128)(2,1)} custom-call(bf16[6,2,6144]{2,1,0:T(2,128)(2,1)} %q_hbm.1, bf16[2,6,16,128]{3,2,1,0:T(8,128)(2,1)} %bitcast.15, bf16[2,6,8,256,128]{4,3,2,1,0:T(8,128)(2,1)} %cache_hbm.1, bf16[6,2,6144]{2,1,0:T(2,128)(2,1)} %res_hbm.1, bf16[384,6144]{1,0:T(8,128)(2,1)} %wout_hbm.1, f32[1,6144]{1,0:T(1,128)} %bitcast.17, ...), custom_call_target="tpu_custom_call" | custom-call | tf_op jit(solution)/shard_map/layer/pallas_call | solution.py:510
  62.0 1.3 %reshape.23 = bf16[6,2,384]{2,1,0:T(2,128)(2,1)} reshape(bf16[12,384]{1,0:T(8,128)(2,1)} %bitcast.16) | data formatting | bytes 18432 | tf_op jit(solution)/shard_map/reshape | solution.py:573

commit v4 on v3

--- a/solution.py
+++ b/solution.py
@@ -54,9 +54,7 @@
     a_send, a_recv, stat, fcol, att, proj, b_send, b_recv,
     state, z_send, z_recv, xall, acc, vacc, hid,
     own, q_send, q_recv, g_send, g_recv, m_send, m_recv, y_send, y_recv,
-    in_sem, kv_sem, w_sem,
-    a_ss, a_rs, b_ss, b_rs, z_ss, z_rs, x1_ss, x1_rs, x2_ss, x2_rs, xp_ss, xp_rs,
-    q_ss, q_rs, g_ss, g_rs, m_ss, m_rs, y_ss, y_rs,
+    in_sem, kv_sem, w_sem, sent, one_rs, z_rs, x1_rs, x2_rs, xp_rs, q_rs, g_rs, m_rs,
 ):
     b = lax.axis_index("expert")
     t = lax.axis_index("tensor")
@@ -76,6 +74,9 @@
         return pltpu.make_async_remote_copy(
             src_ref=src, dst_ref=dst, send_sem=ss, recv_sem=rs, device_id=dev, device_id_type=MESH
         )
+
+    def settle(ref, sem):
+        pltpu.make_async_copy(ref, ref, sem).wait()
 
     inputs = [
         pltpu.make_async_copy(src, dst, in_sem.at[i])
@@ -174,7 +175,7 @@
 
     def a_copy(i):
         to = plane_peer(i)
-        return remote(a_send.at[to], a_recv.at[t], a_ss.at[i], a_rs.at[i], (b, to))
+        return remote(a_send.at[to], a_recv.at[t], sent.at[0], one_rs.at[0], (b, to))
 
     for i in FAR_PLANE:
         a_copy(i).start()
@@ -237,8 +238,7 @@
     att[...] = jnp.zeros_like(att)
     weights_in[0].wait()
 
-    for i in reversed(FAR_PLANE):
-        a_copy(i).wait_recv()
+    settle(a_recv.at[pl.ds(0, 15)], one_rs.at[0])
 
     stats = a_recv[:, 48:64, :].astype(F32)
     tops, totals = stats[:, 0:8], stats[:, 8:16]
@@ -275,15 +275,14 @@
 
     def b_copy(i):
         to = plane_peer(i)
-        return remote(b_send.at[to], b_recv.at[t], b_ss.at[i], b_rs.at[i], (b, to))
+        return remote(b_send.at[to], b_recv.at[t], sent.at[1], one_rs.at[1], (b, to))
 
     for i in FAR_PLANE:
         to = plane_peer(i)
         b_send[to] = (proj[to] + head).astype(BF)
         b_copy(i).start()
     b_recv[t] = (proj[t] + head).astype(BF)
-    for i in reversed(FAR_PLANE):
-        b_copy(i).wait_recv()
+    settle(b_recv.at[pl.ds(0, 15)], one_rs.at[1])
 
     summed = jnp.sum(b_recv[...].astype(F32), axis=0)
     spread = jnp.where(token_row == slot_lane, summed[6:7, 0:128] + summed[7:8, 0:128], 0.0)
@@ -296,7 +295,7 @@
 
     def z_copy(p):
         to = wrap(z + ORDER[p], 8)
-        return remote(z_send.at[to], z_recv.at[p], z_ss.at[p], z_rs.at[p], (2 * to + c, t))
+        return remote(z_send.at[to], z_recv.at[p], sent.at[2], z_rs.at[int(p >= NEAR)], (2 * to + c, t))
 
     for p in range(7, 0, -1):
         z_copy(p).start()
@@ -308,18 +307,17 @@
 
     def x1_copy(j, group):
         part = rows_of(t, group)
-        n = 2 * j + group
-        return remote(part, part, x1_ss.at[n], x1_rs.at[n], (b, place(c, g, wrap(m + j, 4))))
+        n = 2 * (j - 1) + group
+        return remote(part, part, sent.at[3], x1_rs.at[n], (b, place(c, g, wrap(m + j, 4))))
 
     def x2_copy(j, d, group):
         part = rows_of(place(c, g, wrap(m - j, 4)), group)
-        n = 8 * j + 2 * d + group
-        return remote(part, part, x2_ss.at[n], x2_rs.at[n], (b, place(c, wrap(g + d, 4), m)))
+        return remote(part, part, sent.at[4], x2_rs.at[j], (b, place(c, wrap(g + d, 4), m)))
 
     def xp_copy(j, d):
         s = place(c, wrap(g - d, 4), wrap(m - j, 4))
-        n = 4 * j + d
-        return remote(xall.at[c, s], xall.at[c, s], xp_ss.at[n], xp_rs.at[n], (partner, t))
+        late = int(j > 0 and d > 0)
+        return remote(xall.at[c, s], xall.at[c, s], sent.at[5], xp_rs.at[late], (partner, t))
 
     def multiply(offsets):
         found = [4 * wrap(y - i, 4) + wrap(x - j, 4) for i, j in offsets]
@@ -337,9 +335,8 @@
         vacc[...] = squares
 
     for group in range(2):
-        span = range(1, NEAR) if group == 0 else range(NEAR, EXPERTS)
-        for p in span:
-            z_copy(p).wait_recv()
+        came = pl.ds(NEAR, EXPERTS - NEAR) if group else pl.ds(1, NEAR - 1)
+        settle(z_recv.at[came], z_rs.at[group])
         blocks = z_recv[0:NEAR] if group == 0 else z_recv[NEAR:EXPERTS]
         lo, n = GROUPS[group]
         xall[c, t, lo : lo + n] = dot(
@@ -362,23 +359,16 @@
                 x2_copy(j, d, group).start()
             if group:
                 xp_copy(j, 0).start()
+    settle(xall.at[0, pl.ds(0, 3)], x2_rs.at[0])
     for d in FAR_RING:
-        for group in range(2):
-            x2_copy(0, d, group).wait_recv()
         xp_copy(0, d).start()
-    for n in range(4):
-        xp_copy(n, 0).wait_recv()
-    for d in FAR_RING:
-        xp_copy(0, d).wait_recv()
+    settle(xall.at[0, pl.ds(0, 7)], xp_rs.at[0])
     multiply([(0, 0), (0, 1), (0, 2), (0, 3), (1, 0), (2, 0), (3, 0)])
     for j in (1, 3, 2):
+        settle(xall.at[0, pl.ds(0, 3)], x2_rs.at[j])
         for d in FAR_RING:
-            for group in range(2):
-                x2_copy(j, d, group).wait_recv()
             xp_copy(j, d).start()
-    for j in (1, 3, 2):
-        for d in FAR_RING:
-            xp_copy(j, d).wait_recv()
+    settle(xall.at[0, pl.ds(0, 9)], xp_rs.at[1])
     multiply([(i, j) for i in (1, 2, 3) for j in (1, 2, 3)])
 
     inverse = lax.rsqrt(jnp.sum(vacc[...], axis=1, keepdims=True) * (1.0 / D) + EPS)
@@ -392,30 +382,28 @@
 
     def q_copy(j):
         part = pl.ds(4 * j, 4)
-        return remote(q_send.at[part], q_recv.at[part], q_ss.at[j], q_rs.at[j], (partner, t))
+        return remote(q_send.at[part], q_recv.at[part], sent.at[6], q_rs.at[j], (partner, t))
 
     def g_copy(j, d, group):
         n = 3 * j + d - 1
-        k = 2 * n + group
         lo, rows = GROUPS[group]
         part = pl.ds(lo, rows)
         return remote(
-            g_send.at[n, part], g_recv.at[n, part], g_ss.at[k], g_rs.at[k],
+            g_send.at[n, part], g_recv.at[n, part], sent.at[7], g_rs.at[2 * j + group],
             (b, place(c, wrap(g + d, 4), m)),
         )
 
     def m_copy(j, group):
-        k = 2 * j + group
         lo, rows = GROUPS[group]
         part = pl.ds(lo, rows)
         return remote(
-            m_send.at[j, part], m_recv.at[j, part], m_ss.at[k], m_rs.at[k],
+            m_send.at[j, part], m_recv.at[j, part], sent.at[8], m_rs.at[group],
             (b, place(c, g, wrap(m + j, 4))),
         )
 
     def y_copy(p):
         to = wrap(z - ORDER[p], 8)
-        return remote(y_send.at[p], y_recv.at[z], y_ss.at[p], y_rs.at[p], (2 * to + c, t))
+        return remote(y_send.at[p], y_recv.at[z], sent.at[9], one_rs.at[2], (2 * to + c, t))
 
     for j in MEMBERS:
         found = [place(1 - c, wrap(m + d, 4), wrap(g + j, 4)) for d in range(4)]
@@ -443,8 +431,8 @@
         lo, n = GROUPS[group]
         for j in MEMBERS:
             whole = own[4 * j, lo : lo + n] + q_recv[4 * j, lo : lo + n].astype(F32)
+            settle(g_recv.at[pl.ds(0, 3), pl.ds(lo, n)], g_rs.at[2 * j + group])
             for d in FAR_RING:
-                g_copy(j, d, group).wait_recv()
                 whole = whole + g_recv[3 * j + d - 1, lo : lo + n].astype(F32)
             if j:
                 m_send[j, lo : lo + n] = whole.astype(BF)
@@ -455,8 +443,8 @@
     for group in (1, 0):
         lo, n = GROUPS[group]
         final = finals[group]
+        settle(m_recv.at[pl.ds(0, 3), pl.ds(lo, n)], m_rs.at[group])
         for j in (1, 3, 2):
-            m_copy(j, group).wait_recv()
             final = final + m_recv[j, lo : lo + n].astype(F32)
         back = dot(unpacking[group], final.astype(BF)).astype(BF)
         if group:
@@ -469,31 +457,21 @@
                 y_copy(p).start()
             y_recv[z] = y_send[0]
 
-    for i in FAR_PLANE:
-        a_copy(i).wait_send()
-        b_copy(i).wait_send()
-    for p in range(1, 8):
-        z_copy(p).wait_send()
-    for j in range(4):
-        q_copy(j).wait_send()
-        for d in range(4):
-            xp_copy(j, d).wait_send()
-    for group in range(2):
-        for j in FAR_RING:
-            x1_copy(j, group).wait_send()
-            m_copy(j, group).wait_send()
-        for j in range(4):
-            for d in FAR_RING:
-                x2_copy(j, d, group).wait_send()
-                g_copy(j, d, group).wait_send()
-
-    for p in range(1, 8):
-        y_copy(p).wait_recv()
+    settle(a_send.at[pl.ds(0, 15)], sent.at[0])
+    settle(b_send.at[pl.ds(0, 15)], sent.at[1])
+    settle(z_send.at[pl.ds(0, 7)], sent.at[2])
+    settle(xall.at[0, pl.ds(0, 3)], sent.at[3])
+    settle(xall.at[0, pl.ds(0, 12)], sent.at[4])
+    settle(xall.at[0], sent.at[5])
+    settle(q_send, sent.at[6])
+    settle(g_send, sent.at[7])
+    settle(m_send.at[pl.ds(0, 3)], sent.at[8])
+
+    settle(y_recv.at[pl.ds(0, 7)], one_rs.at[2])
     returned = y_recv[...].reshape(128, PART)
     mix = dot(combine_high, returned) + dot(combine_low, returned)
     out_ref[...] = (state[...] + mix).astype(BF)
-    for p in range(1, 8):
-        y_copy(p).wait_send()
+    settle(y_send.at[pl.ds(0, 7)], sent.at[9])
 
 
 def body(queries, new_kv, cache, residual, w_out, norm_gain, routes, route_weight, w_in, w_down):
@@ -551,19 +529,8 @@
             vmem((4, PACK, PART), BF),
             vmem((EXPERTS, 16, PART), BF),
             vmem((EXPERTS, 16, PART), BF),
-            dma((6,)),
-            dma((2, ROWS)),
-            dma((3,)),
-            dma((16,)), dma((16,)),
-            dma((16,)), dma((16,)),
-            dma((8,)), dma((8,)),
-            dma((8,)), dma((8,)),
-            dma((32,)), dma((32,)),
-            dma((16,)), dma((16,)),
-            dma((4,)), dma((4,)),
-            dma((24,)), dma((24,)),
-            dma((8,)), dma((8,)),
-            dma((8,)), dma((8,)),
+            dma((6,)), dma((2, ROWS)), dma((3,)), dma((10,)), dma((3,)),
+            dma((2,)), dma((6,)), dma((4,)), dma((2,)), dma((4,)), dma((8,)), dma((2,)),
         ],
         compiler_params=pltpu.CompilerParams(
             collective_id=0, has_side_effects=True, vmem_limit_bytes=56 * 1024 * 1024

time: 63.5 us -> 61.3 us (0.965)
  Pallas kernels: 62 us -> 59.8 us
    pallas_call x1, Pallas kernels: 62 us -> 59.8 us  [body(): pl.pallas_call(kernel, out_shape=jax.ShapeDtypeStruct((16, PART), BF), in...]
where the time goes in v4:
time: 61.3 us; the launch traced here: 61.2 us
  Pallas kernels  59.8 us (98%)
  local copies, waits for them, and re-layouts  1.32 us (2%)
    pallas_call x1, Pallas kernels, body(): pl.pallas_call(kernel, out_shape=jax.ShapeDtypeStruct((16, PART), BF), in...  59.8 us
    reshape x1, local copies, waits for them, and re-layouts, body(): return out[:12].reshape(ROWS, STEPS, PART)  1.32 us

profile of v4, /device:TPU:6, one launch (start us, length us, event | category | flops | bytes accessed | tf_op | source)
XLA Modules:
  0.0 61.2 jit_solution(10060300663693516652)
XLA Ops:
  0.0 59.8 %layer.1 = bf16[16,384]{1,0:T(8,128)(2,1)} custom-call(bf16[6,2,6144]{2,1,0:T(2,128)(2,1)} %q_hbm.1, bf16[2,6,16,128]{3,2,1,0:T(8,128)(2,1)} %bitcast.15, bf16[2,6,8,256,128]{4,3,2,1,0:T(8,128)(2,1)} %cache_hbm.1, bf16[6,2,6144]{2,1,0:T(2,128)(2,1)} %res_hbm.1, bf16[384,6144]{1,0:T(8,128)(2,1)} %wout_hbm.1, f32[1,6144]{1,0:T(1,128)} %bitcast.17, ...), custom_call_target="tpu_custom_call" | custom-call | tf_op jit(solution)/shard_map/layer/pallas_call | solution.py:488
  59.9 1.3 %reshape.23 = bf16[6,2,384]{2,1,0:T(2,128)(2,1)} reshape(bf16[12,384]{1,0:T(8,128)(2,1)} %bitcast.16) | data formatting | bytes 18432 | tf_op jit(solution)/shard_map/reshape | solution.py:540

commit v5 on v4

--- a/solution.py
+++ b/solution.py
@@ -27,9 +27,9 @@
 FAR_PLANE = (10, 6, 9, 11, 14, 2, 8, 5, 7, 13, 15, 1, 3, 4, 12)
 FAR_RING = (2, 1, 3)
 ORDER = (0, 1, 7, 2, 6, 3, 5, 4)
-NEAR = 5
-GROUPS = ((0, 48), (48, 32))
-MEMBERS = (2, 1, 3, 0)
+NEAR = 3
+GROUPS = ((0, 32), (32, 48))
+MEMBERS = (1, 3, 2, 0)
 
 
 def wrap(value, size):
@@ -82,7 +82,7 @@
         pltpu.make_async_copy(src, dst, in_sem.at[i])
         for i, (src, dst) in enumerate(
             [
-                (q_hbm, q_raw), (nkv_hbm, nkv), (res_hbm, res_raw), (gain_hbm, gain_ref),
+                (q_hbm, q_raw), (nkv_hbm, nkv.at[:, :, pl.ds(0, 16)]), (res_hbm, res_raw), (gain_hbm, gain_ref),
                 (routes_hbm, routes_raw), (rw_hbm, rw_raw),
             ]
         )
@@ -100,10 +100,11 @@
         pltpu.make_async_copy(wdn_hbm, wdn, w_sem.at[2]),
     ]
     inputs[0].start()
-    inputs[1].start()
     for pair in rows_in[:3]:
         for copy in pair:
             copy.start()
+    nkv[...] = jnp.zeros_like(nkv)
+    inputs[1].start()
 
     barrier = pltpu.get_barrier_semaphore()
 
@@ -129,12 +130,19 @@
         q_ref[r] = jnp.concatenate(pieces, axis=0).astype(BF)
     inputs[1].wait()
 
-    row_id = iota((128, 16), 0)
-    key_id = iota((128, 16), 1)
+    def a_copy(i, half):
+        to = plane_peer(i)
+        part = pl.ds(32 * half, 32)
+        return remote(
+            a_send.at[to, part], a_recv.at[t, part], sent.at[0], one_rs.at[0], (b, to)
+        )
+
+    row_id = iota((128, 128), 0)
+    key_id = iota((128, 128), 1)
     fresh_ok = (
         (lax.div(row_id, 16) == lax.div(key_id, 2))
         & (lax.rem(key_id, 2) <= lax.rem(row_id, 2))
-        & (jnp.broadcast_to(t, (128, 16)) == 0)
+        & (jnp.broadcast_to(t, (128, 128)) == 0)
     )
     lane = iota((128, 128), 1)
     tallies = jnp.zeros((128, 128), F32)
@@ -154,13 +162,12 @@
             ) * (HD**-0.5)
             extra = dot(qr, nkv[0, r], NT) * (HD**-0.5)
             extra = jnp.where(fresh_ok, extra, -jnp.inf)
-            top = jnp.maximum(
-                jnp.max(scores, axis=1, keepdims=True), jnp.max(extra, axis=1, keepdims=True)
-            )
-            top = jnp.ceil(top * 0.25) * 4.0
+            top = jnp.maximum(jnp.maximum(scores[:, 0:128], scores[:, 128:256]), extra)
+            top = jnp.ceil(jnp.max(top, axis=1, keepdims=True) * 0.25) * 4.0
             weights = jnp.exp(scores - top)
             extra = jnp.exp(extra - top)
-            total = jnp.sum(weights, axis=1, keepdims=True) + jnp.sum(extra, axis=1, keepdims=True)
+            total = weights[:, 0:128] + weights[:, 128:256] + extra
+            total = jnp.sum(total, axis=1, keepdims=True)
             low = weights.astype(BF)
             rows_in[r][1].wait()
             mixed = jnp.concatenate(
@@ -169,16 +176,14 @@
             tallies = jnp.where(lane == r, top, jnp.where(lane == 8 + r, total, tallies))
             halves.append(mixed.reshape(16, 8, 128))
         a_send[:, 16 * pair : 16 * pair + 16, :] = jnp.concatenate(halves, axis=1).astype(BF)
+        if pair == 1:
+            pl.semaphore_wait(barrier, 23)
+            for i in FAR_PLANE:
+                a_copy(i, 0).start()
     table = jnp.transpose(tallies)[0:16, :].astype(BF)
     a_send[:, 48:64, :] = jnp.broadcast_to(table[None], (16, 16, 128))
-    pl.semaphore_wait(barrier, 23)
-
-    def a_copy(i):
-        to = plane_peer(i)
-        return remote(a_send.at[to], a_recv.at[t], sent.at[0], one_rs.at[0], (b, to))
-
     for i in FAR_PLANE:
-        a_copy(i).start()
+        a_copy(i, 1).start()
     a_recv[t] = a_send[t]
     weights_in[1].start()
     weights_in[2].start()
@@ -262,11 +267,12 @@
                     ]
 
     attended = att[...].astype(BF)
-    proj_sum = jnp.zeros((16, 1), F32)
+    proj_sum = jnp.zeros((16, 128), F32)
     for s in range(16):
         part = dot(attended, wout[:, PART * s : PART * s + PART])
         proj[s] = part
-        proj_sum = proj_sum + jnp.sum(part, axis=1, keepdims=True)
+        proj_sum = proj_sum + part[:, 0:128] + part[:, 128:256] + part[:, 256:384]
+    proj_sum = jnp.sum(proj_sum, axis=1, keepdims=True)
     diagonal = jnp.sum(jnp.where(token_row == slot_lane, proj_sum, 0.0), axis=0, keepdims=True)
     high = diagonal.astype(BF).astype(F32)
     low = diagonal - high
@@ -449,11 +455,11 @@
         back = dot(unpacking[group], final.astype(BF)).astype(BF)
         if group:
             y_send[NEAR:EXPERTS] = back.reshape(EXPERTS - NEAR, 16, PART)
-            for p in (7, 6, 5):
+            for p in range(7, NEAR - 1, -1):
                 y_copy(p).start()
         else:
             y_send[0:NEAR] = back.reshape(NEAR, 16, PART)
-            for p in (4, 3, 2, 1):
+            for p in range(NEAR - 1, 0, -1):
                 y_copy(p).start()
             y_recv[z] = y_send[0]
 
@@ -492,7 +498,7 @@
         out_specs=pl.BlockSpec(memory_space=pltpu.VMEM),
         scratch_shapes=[
             vmem((ROWS, STEPS, D), BF),
-            vmem((2, ROWS, 16, HD), BF),
+            vmem((2, ROWS, 128, HD), BF),
             vmem((ROWS, STEPS, D), BF),
             vmem((1, D), F32),
             vmem((STEPS, TOP, ROWS), jnp.int32),

time: 61.3 us -> 60.4 us (0.985); the launches traced: 61.2 us -> 59.4 us
  Pallas kernels: 59.8 us -> 58.1 us
    pallas_call x1, Pallas kernels: 59.8 us -> 58.1 us  [body(): pl.pallas_call(kernel, out_shape=jax.ShapeDtypeStruct((16, PART), BF), in...]
where the time goes in v5:
time: 60.4 us; the launch traced here: 59.4 us
  Pallas kernels  58.1 us (96%)
  local copies, waits for them, and re-layouts  1.32 us (2%)
    pallas_call x1, Pallas kernels, body(): pl.pallas_call(kernel, out_shape=jax.ShapeDtypeStruct((16, PART), BF), in...  58.1 us
    reshape x1, local copies, waits for them, and re-layouts, body(): return out[:12].reshape(ROWS, STEPS, PART)  1.32 us

profile of v5, /device:TPU:6, one launch (start us, length us, event | category | flops | bytes accessed | tf_op | source)
XLA Modules:
  0.0 59.4 jit_solution(7166548603577037469)
XLA Ops:
  0.0 58.1 %layer.1 = bf16[16,384]{1,0:T(8,128)(2,1)} custom-call(bf16[6,2,6144]{2,1,0:T(2,128)(2,1)} %q_hbm.1, bf16[2,6,16,128]{3,2,1,0:T(8,128)(2,1)} %bitcast.15, bf16[2,6,8,256,128]{4,3,2,1,0:T(8,128)(2,1)} %cache_hbm.1, bf16[6,2,6144]{2,1,0:T(2,128)(2,1)} %res_hbm.1, bf16[384,6144]{1,0:T(8,128)(2,1)} %wout_hbm.1, f32[1,6144]{1,0:T(1,128)} %bitcast.17, ...), custom_call_target="tpu_custom_call" | custom-call | tf_op jit(solution)/shard_map/layer/pallas_call | solution.py:494
  58.1 1.3 %reshape.23 = bf16[6,2,384]{2,1,0:T(2,128)(2,1)} reshape(bf16[12,384]{1,0:T(8,128)(2,1)} %bitcast.16) | data formatting | bytes 18432 | tf_op jit(solution)/shard_map/reshape | solution.py:546
